TPU v7x, 128 devices: a whole 4x4x4 slice. The times are simulated.
128 devices in a mesh: dp: 16 (over z_hi, y, core), blk: 8 (over x, z_lo).
Axes of the slice: x: 4, y: 4, z: 4 (z_hi: 2, z_lo: 2; z = z_hi * 2 + z_lo), core: 2. Of those that a mesh axis runs over, the one named last changes fastest.
Arguments:
- queries: bfloat16 [24576, 4096], P(('dp', 'blk')), parts along dimension 0
- keys: bfloat16 [24576, 1024], P(('dp', 'blk')), parts along dimension 0
- values: bfloat16 [24576, 1024], P(('dp', 'blk')), parts along dimension 0, may hold values from -6 to 6
- outputs: bfloat16 [24576, 4096], P(('dp', 'blk')), parts along dimension 0, may hold values from -3 to 3
- output_gradient: bfloat16 [24576, 4096], P(('dp', 'blk')), parts along dimension 0, may hold values from -6 to 6
- doc_ids: int32 [24576], P(('dp', 'blk')), parts along dimension 0, may hold values from 0 to 7, as said below
Outputs:
- query_grad: bfloat16 [24576, 4096], P(('dp', 'blk')), parts along dimension 0
- gradient_of_keys: bfloat16 [24576, 1024], P(('dp', 'blk')), parts along dimension 0
- gradient_of_values: bfloat16 [24576, 1024], P(('dp', 'blk')), parts along dimension 0
There are 16 independent parts, one for each index of `dp`. A program takes and returns all parts, laid end to end along the dimension named above; each array names one. Nothing has to cross between parts.
Inputs may be any that keep to these rules, and one draw needn't show every extreme that they name: `doc_ids`: document numbers never fall along the sequence; every document holds at most 768 tokens and one holds exactly 768.
All inputs are finite; a program needn't handle non-finite values.
Results may differ from a plain program's by a relative error of at most 0.007.
Values may be sent and summed in bfloat16 or wider, within the bound.
No kernel may reach another device: no remote copies, remote signals or barrier semaphores. Data moves between devices by JAX's collectives and lax.ppermute only.
A program may use at most 192 MiB of HBM per device.

v0:
```python
import math

import jax
import jax.numpy as jnp
from jax import lax
from jax.sharding import PartitionSpec as P

QUERY_HEADS = 32
KEY_VALUE_HEADS = 8
HEAD_WIDTH = 128


def from_behind(value, axis, steps):
    count = lax.axis_size(axis)
    pairs = [(source, (source + steps) % count) for source in range(count)]
    return lax.ppermute(value, axis, pairs)


def from_behind_2(block, axis, distance):
    devices = range(lax.axis_size(axis))
    route = [(i - distance, i) for i in devices if i - distance in devices]
    return lax.ppermute(block, axis, route)


def local(queries, keys, values, outputs, output_gradient, doc_ids):
    count_of_rows = queries.shape[0]
    group_width = QUERY_HEADS // KEY_VALUE_HEADS
    scale_for_scores = 1.0 / math.sqrt(HEAD_WIDTH)
    block_count = lax.axis_size("blk")
    own_index = lax.axis_index("blk")
    query_pos = own_index * count_of_rows + jnp.arange(count_of_rows, dtype=jnp.int32)
    head_queries = queries.reshape(count_of_rows, KEY_VALUE_HEADS, group_width, HEAD_WIDTH)
    gradient_head_rows = output_gradient.reshape(
        count_of_rows, KEY_VALUE_HEADS, group_width, HEAD_WIDTH
    )
    product = (output_gradient.astype(jnp.float32) * outputs.astype(jnp.float32)).reshape(
        count_of_rows, KEY_VALUE_HEADS, group_width, HEAD_WIDTH
    )
    row_delta = jnp.transpose(jnp.sum(product, axis=3), (1, 2, 0))

    def mask_for(seg_block, first_row, usable):
        key_pos = first_row + jnp.arange(seg_block.shape[0], dtype=jnp.int32)
        same_doc = doc_ids[:, None] == seg_block[None, :]
        return same_doc & (key_pos[None, :] <= query_pos[:, None]) & usable

    def key_scores(block_of_keys):
        rows_of_keys = block_of_keys.reshape(block_of_keys.shape[0], KEY_VALUE_HEADS, HEAD_WIDTH)
        return (
            jnp.einsum(
                "qhgd,khd->hgqk", head_queries, rows_of_keys, preferred_element_type=jnp.float32
            )
            * scale_for_scores
        )

    initial = (
        jnp.full((KEY_VALUE_HEADS, group_width, count_of_rows), -1e30, jnp.float32),
        jnp.zeros((KEY_VALUE_HEADS, group_width, count_of_rows), jnp.float32),
    )
    query_gradient_total = jnp.zeros(
        (count_of_rows, KEY_VALUE_HEADS, group_width, HEAD_WIDTH), jnp.float32
    )
    first_row = jnp.int32(0)
    stats_block_of_keys = lax.all_gather(keys, "blk", axis=0, tiled=True)
    usable = first_row >= 0
    allowed = mask_for(lax.all_gather(doc_ids, "blk", axis=0, tiled=True), first_row, usable)

    def update(current):
        run_max, run_sum = current
        masked = jnp.where(allowed, key_scores(stats_block_of_keys), -1e30)
        new_max = jnp.maximum(run_max, jnp.max(masked, axis=3))
        added = jnp.sum(jnp.where(allowed, jnp.exp(masked - new_max[..., None]), 0.0), axis=3)
        return (new_max, added)

    running = lax.cond(jnp.any(allowed), update, lambda current: current, initial)
    lse = running[0] + jnp.log(running[1])
    block_of_keys, block_of_values, seg_block = (keys, values, doc_ids)
    key_gradient_total = jnp.zeros((count_of_rows, KEY_VALUE_HEADS, HEAD_WIDTH), jnp.float32)
    value_gradient_total = jnp.zeros((count_of_rows, KEY_VALUE_HEADS, HEAD_WIDTH), jnp.float32)
    for travel in range(block_count):
        anchor = own_index - travel
        grads_allowed = mask_for(seg_block, anchor * count_of_rows, anchor >= 0)
        grads_rows_of_keys = block_of_keys.reshape(
            block_of_keys.shape[0], KEY_VALUE_HEADS, HEAD_WIDTH
        )
        rows_of_values = block_of_values.reshape(
            block_of_values.shape[0], KEY_VALUE_HEADS, HEAD_WIDTH
        )

        def compute(unused):
            scores = key_scores(block_of_keys)
            probs = jnp.exp(jnp.where(grads_allowed, scores - lse[..., None], -1e30))
            probs_low = probs.astype(jnp.bfloat16)
            value_part = jnp.einsum(
                "hgqk,qhgd->khd", probs_low, gradient_head_rows, preferred_element_type=jnp.float32
            )
            prob_grad = jnp.einsum(
                "qhgd,khd->hgqk",
                gradient_head_rows,
                rows_of_values,
                preferred_element_type=jnp.float32,
            )
            score_grad = (probs * (prob_grad - row_delta[..., None])).astype(jnp.bfloat16)
            query_part = jnp.einsum(
                "hgqk,khd->qhgd", score_grad, grads_rows_of_keys, preferred_element_type=jnp.float32
            )
            key_part = jnp.einsum(
                "hgqk,qhgd->khd", score_grad, head_queries, preferred_element_type=jnp.float32
            )
            return (query_part, key_part, value_part)

        def blank(unused):
            return (
                jnp.zeros((count_of_rows, KEY_VALUE_HEADS, group_width, HEAD_WIDTH), jnp.float32),
                jnp.zeros(grads_rows_of_keys.shape, jnp.float32),
                jnp.zeros(rows_of_values.shape, jnp.float32),
            )

        query_part, key_part, value_part = lax.cond(jnp.any(grads_allowed), compute, blank, 0)
        query_gradient_total = query_gradient_total + query_part
        key_gradient_total, value_gradient_total = from_behind(
            (key_gradient_total + key_part, value_gradient_total + value_part), "blk", 1
        )
        if travel + 1 < block_count:
            block_of_keys, block_of_values, seg_block = from_behind_2(
                (block_of_keys, block_of_values, seg_block), "blk", 1
            )
    query_grad = (
        (query_gradient_total * scale_for_scores)
        .reshape(count_of_rows, QUERY_HEADS * HEAD_WIDTH)
        .astype(jnp.bfloat16)
    )
    gradient_of_keys = (
        (key_gradient_total * scale_for_scores)
        .reshape(count_of_rows, KEY_VALUE_HEADS * HEAD_WIDTH)
        .astype(jnp.bfloat16)
    )
    gradient_of_values = value_gradient_total.reshape(
        count_of_rows, KEY_VALUE_HEADS * HEAD_WIDTH
    ).astype(jnp.bfloat16)
    return (query_grad, gradient_of_keys, gradient_of_values)


def solution(mesh):
    placed = (
        P(("dp", "blk"), None),
        P(("dp", "blk"), None),
        P(("dp", "blk"), None),
        P(("dp", "blk"), None),
        P(("dp", "blk"), None),
        P(("dp", "blk")),
    )
    return jax.shard_map(
        local,
        mesh=mesh,
        in_specs=placed,
        out_specs=(P(("dp", "blk"), None), P(("dp", "blk"), None), P(("dp", "blk"), None)),
        check_vma=False,
    )
```

profile of v0, /device:TPU:0, one launch (start us, length us, event | category | flops | bytes accessed | tf_op | source)
XLA Modules:
  0.0 659.6 jit_solution(6816807608785728740)
XLA Ops:
  14.6 11.8 %all-reduce = s32[1536]{0:T(1024)S(1)} all-reduce(s32[1536]{0:T(1024)S(1)} %dynamic-update-slice), channel_id=1, replica_groups=mesh['dp'=16,'blk'=8] {'blk'}, use_global_device_ids=true, to_apply=%add | all-reduce | flops 1536 | bytes 12288
  68.8 13.5 %all-gather.2.cloned.1.call-done = bf16[1536,1024]{1,0:T(8,128)(2,1)} async-done(((bf16[192,1024]{1,0:T(8,128)(2,1)}), bf16[1536,1024]{1,0:T(8,128)(2,1)}) %all-gather.2.cloned.1.call-update) | async-done | bytes 3145744 | tf_op jit(solution)/shard_map/all_gather | solution.py:63
  82.3 41.0 %conditional.9 = (f32[8,4,192]{2,1,0:T(4,128)}, f32[8,4,192]{2,1,0:T(4,128)S(1)}) conditional(s32[]{:T(128)} %convert_element_type.100, () %tuple.83, (pred[192,1536]{1,0:T(8,128)(4,1)S(1)}, bf16[1536,1024]{1,0:T(8,128)(2,1)}, bf16[192,8,4,128]{3,2,1,0:T(4,128)(2,1)S(1)}) %tuple.84), branch_computations={%region_2.0_spmd, %region_3.6_spmd} | conditional | flops 2491410432 | bytes 87269392 | solution.py:74
  86.9 18.5 %fusion = (f32[8,4,192]{2,1,0:T(4,128)S(1)}, f32[8,1536,192,4]{1,2,3,0:T(8,128)}) fusion(pred[192,1536]{1,0:T(8,128)(4,1)S(1)} %get-tuple-element.142, bf16[192,8,4,128]{3,2,1,0:T(4,128)(2,1)S(1)} %get-tuple-element.321, bf16[1536,8,128,1]{2,1,0,3:T(8,128)(2,1)} %bitcast.371), kind=kOutput, calls=%fused_computation.2 | convolution fusion | flops 2444224512 | bytes 42786816 | tf_op jit(solution)/shard_map/cond/branch_1_fun/qhgd,khd->hgqk/dot_general | solution.py:49
  106.0 17.3 %select_reduce_fusion = f32[8,4,192]{2,1,0:T(4,128)S(1)} fusion(f32[8,1536,192,4]{1,2,3,0:T(8,128)} %get-tuple-element.394, f32[8,4,192]{2,1,0:T(4,128)} %broadcast_maximum_fusion, pred[192,1536]{1,0:T(8,128)(4,1)S(1)} %get-tuple-element.142), kind=kLoop, calls=%fused_computation.1 | loop fusion | flops 47179776 | bytes 38092800 | tf_op jit(solution)/shard_map/cond/branch_1_fun/reduce_sum | solution.py:71
  124.1 20.0 %conditional.10 = (f32[192,8,4,128]{3,0,2,1:T(8,128)}, f32[192,8,128]{2,0,1:T(8,128)}, f32[192,8,128]{2,0,1:T(8,128)}) conditional(s32[]{:T(128)} %convert_element_type.99, () %tuple.82, (pred[192,192]{0,1:T(8,128)(4,1)S(1)}, bf16[192,1024]{1,0:T(8,128)(2,1)S(1)}, bf16[192,8,4,128]{3,2,1,0:T(4,128)(2,1)S(1)}, f32[8,4,192]{2,1,0:T(4,128)S(1)}, ...), branch_computations={%region_7.8_spmd, %region_8.9_spmd} | conditional | flops 1521745920 | bytes 61145188 | solution.py:118
  129.3 5.9 fusion.5
  155.3 33.5 %collective-permute-done.1 = bf16[192,1024]{1,0:T(8,128)(2,1)} collective-permute-done((bf16[192,1024]{1,0:T(8,128)(2,1)S(1)}, bf16[192,1024]{1,0:T(8,128)(2,1)}, u32[]{:S(2)}, u32[]{:S(2)}) %collective-permute-start.1) | collective-permute-done | bytes 393248 | tf_op jit(solution)/shard_map/ppermute | solution.py:22
  188.8 6.6 %collective-permute-done.2 = bf16[192,1024]{1,0:T(8,128)(2,1)} collective-permute-done((bf16[192,1024]{1,0:T(8,128)(2,1)S(1)}, bf16[192,1024]{1,0:T(8,128)(2,1)}, u32[]{:S(2)}, u32[]{:S(2)}) %collective-permute-start.2) | collective-permute-done | bytes 393248 | tf_op jit(solution)/shard_map/ppermute | solution.py:22
  201.4 22.3 %collective-permute-start.30 = (f32[192,8,128]{2,0,1:T(8,128)}, f32[192,8,128]{2,0,1:T(8,128)}, u32[]{:S(2)}, u32[]{:S(2)}) collective-permute-start(f32[192,8,128]{2,0,1:T(8,128)} %add.190), channel_id=1, source_target_pairs={{0,1},{1,2},{2,3},{3,4},{4,5},{5,6},{6,7},{7,0},{8,9},{9,10},{10,1... | collective-permute-start | bytes 2359304 | tf_op jit(solution)/shard_map/ppermute | solution.py:16
  237.4 29.9 %collective-permute-done.4 = bf16[192,1024]{1,0:T(8,128)(2,1)} collective-permute-done((bf16[192,1024]{1,0:T(8,128)(2,1)}, bf16[192,1024]{1,0:T(8,128)(2,1)}, u32[]{:S(2)}, u32[]{:S(2)}) %collective-permute-start.4) | collective-permute-done | bytes 393248 | tf_op jit(solution)/shard_map/ppermute | solution.py:22
  267.3 6.6 %collective-permute-done.5 = bf16[192,1024]{1,0:T(8,128)(2,1)} collective-permute-done((bf16[192,1024]{1,0:T(8,128)(2,1)}, bf16[192,1024]{1,0:T(8,128)(2,1)}, u32[]{:S(2)}, u32[]{:S(2)}) %collective-permute-start.5) | collective-permute-done | bytes 393248 | tf_op jit(solution)/shard_map/ppermute | solution.py:22
  285.0 23.0 %collective-permute-start.23 = (f32[192,8,128]{2,0,1:T(8,128)}, f32[192,8,128]{2,0,1:T(8,128)}, u32[]{:S(2)}, u32[]{:S(2)}) collective-permute-start(f32[192,8,128]{2,0,1:T(8,128)} %add.184), channel_id=1, source_target_pairs={{0,1},{1,2},{2,3},{3,4},{4,5},{5,6},{6,7},{7,0},{8,9},{9,10},{10,1... | collective-permute-start | bytes 2359304 | tf_op jit(solution)/shard_map/ppermute | solution.py:16
  316.2 18.6 %collective-permute-done.7 = bf16[192,1024]{1,0:T(8,128)(2,1)} collective-permute-done((bf16[192,1024]{1,0:T(8,128)(2,1)}, bf16[192,1024]{1,0:T(8,128)(2,1)}, u32[]{:S(2)}, u32[]{:S(2)}) %collective-permute-start.7) | collective-permute-done | bytes 393248 | tf_op jit(solution)/shard_map/ppermute | solution.py:22
  334.8 5.4 collective-permute-done.8
  345.9 15.0 %collective-permute-start.32 = (f32[192,8,128]{2,0,1:T(8,128)}, f32[192,8,128]{2,0,1:T(8,128)}, u32[]{:S(2)}, u32[]{:S(2)}) collective-permute-start(f32[192,8,128]{2,0,1:T(8,128)} %add.192), channel_id=1, source_target_pairs={{0,1},{1,2},{2,3},{3,4},{4,5},{5,6},{6,7},{7,0},{8,9},{9,10},{10,1... | collective-permute-start | bytes 2359304 | tf_op jit(solution)/shard_map/ppermute | solution.py:16
  366.4 21.9 %collective-permute-start.10 = (bf16[192,1024]{1,0:T(8,128)(2,1)}, bf16[192,1024]{1,0:T(8,128)(2,1)}, u32[]{:S(2)}, u32[]{:S(2)}) collective-permute-start(bf16[192,1024]{1,0:T(8,128)(2,1)} %collective-permute-done.7), channel_id=1, source_target_pairs={{0,1},{1,2},{2,3},{3,4},{4,5},{5,6},{6,7},{8,9},{9,10},{10,11},{11... | collective-permute-start | bytes 1179656 | tf_op jit(solution)/shard_map/ppermute | solution.py:22
  388.2 5.3 collective-permute-start.11
  394.2 10.3 %collective-permute-done.10 = bf16[192,1024]{1,0:T(8,128)(2,1)} collective-permute-done((bf16[192,1024]{1,0:T(8,128)(2,1)}, bf16[192,1024]{1,0:T(8,128)(2,1)}, u32[]{:S(2)}, u32[]{:S(2)}) %collective-permute-start.10) | collective-permute-done | bytes 393248 | tf_op jit(solution)/shard_map/ppermute | solution.py:22
  415.1 7.6 %collective-permute-start.33 = (f32[192,8,128]{2,0,1:T(8,128)}, f32[192,8,128]{2,0,1:T(8,128)}, u32[]{:S(2)}, u32[]{:S(2)}) collective-permute-start(f32[192,8,128]{2,0,1:T(8,128)} %add.193), channel_id=1, source_target_pairs={{0,1},{1,2},{2,3},{3,4},{4,5},{5,6},{6,7},{7,0},{8,9},{9,10},{10,1... | collective-permute-start | bytes 2359304 | tf_op jit(solution)/shard_map/ppermute | solution.py:16
  424.8 15.0 %collective-permute-start.25 = (f32[192,8,128]{2,0,1:T(8,128)}, f32[192,8,128]{2,0,1:T(8,128)}, u32[]{:S(2)}, u32[]{:S(2)}) collective-permute-start(f32[192,8,128]{2,0,1:T(8,128)} %add.186), channel_id=1, source_target_pairs={{0,1},{1,2},{2,3},{3,4},{4,5},{5,6},{6,7},{7,0},{8,9},{9,10},{10,1... | collective-permute-start | bytes 2359304 | tf_op jit(solution)/shard_map/ppermute | solution.py:16
  439.8 6.1 collective-permute-start.13
  445.9 24.9 %collective-permute-start.14 = (bf16[192,1024]{1,0:T(8,128)(2,1)}, bf16[192,1024]{1,0:T(8,128)(2,1)}, u32[]{:S(2)}, u32[]{:S(2)}) collective-permute-start(bf16[192,1024]{1,0:T(8,128)(2,1)} %collective-permute-done.11), channel_id=1, source_target_pairs={{0,1},{1,2},{2,3},{3,4},{4,5},{5,6},{6,7},{8,9},{9,10},{10,11},{11... | collective-permute-start | bytes 1179656 | tf_op jit(solution)/shard_map/ppermute | solution.py:22
  481.3 9.5 %collective-permute-start.34 = (f32[192,8,128]{2,0,1:T(8,128)}, f32[192,8,128]{2,0,1:T(8,128)}, u32[]{:S(2)}, u32[]{:S(2)}) collective-permute-start(f32[192,8,128]{2,0,1:T(8,128)} %add.194), channel_id=1, source_target_pairs={{0,1},{1,2},{2,3},{3,4},{4,5},{5,6},{6,7},{7,0},{8,9},{9,10},{10,1... | collective-permute-start | bytes 2359304 | tf_op jit(solution)/shard_map/ppermute | solution.py:16
  493.0 11.4 %collective-permute-start.26 = (f32[192,8,128]{2,0,1:T(8,128)}, f32[192,8,128]{2,0,1:T(8,128)}, u32[]{:S(2)}, u32[]{:S(2)}) collective-permute-start(f32[192,8,128]{2,0,1:T(8,128)} %add.187), channel_id=1, source_target_pairs={{0,1},{1,2},{2,3},{3,4},{4,5},{5,6},{6,7},{7,0},{8,9},{9,10},{10,1... | collective-permute-start | bytes 2359304 | tf_op jit(solution)/shard_map/ppermute | solution.py:16
  504.4 17.7 %collective-permute-start.16 = (bf16[192,1024]{1,0:T(8,128)(2,1)}, bf16[192,1024]{1,0:T(8,128)(2,1)}, u32[]{:S(2)}, u32[]{:S(2)}) collective-permute-start(bf16[192,1024]{1,0:T(8,128)(2,1)} %collective-permute-done.13), channel_id=1, source_target_pairs={{0,1},{1,2},{2,3},{3,4},{4,5},{5,6},{6,7},{8,9},{9,10},{10,11},{11... | collective-permute-start | bytes 1179656 | tf_op jit(solution)/shard_map/ppermute | solution.py:22
  528.7 9.5 %collective-permute-done.15 = s32[192]{0:T(256)S(1)} collective-permute-done((s32[192]{0:T(256)S(1)}, s32[192]{0:T(256)S(1)}, u32[]{:S(2)}, u32[]{:S(2)}) %collective-permute-start.15) | collective-permute-done | bytes 800 | tf_op jit(solution)/shard_map/ppermute | solution.py:22
  538.2 12.6 %collective-permute-start.18 = (s32[192]{0:T(256)S(1)}, s32[192]{0:T(256)S(1)}, u32[]{:S(2)}, u32[]{:S(2)}) collective-permute-start(s32[192]{0:T(256)S(1)} %collective-permute-done.15), channel_id=1, source_target_pairs={{0,1},{1,2},{2,3},{3,4},{4,5},{5,6},{6,7},{8,9},{9,10},{10,11},{11... | collective-permute-start | bytes 2312 | tf_op jit(solution)/shard_map/ppermute | solution.py:22
  560.0 15.0 %collective-permute-start.35 = (f32[192,8,128]{2,0,1:T(8,128)}, f32[192,8,128]{2,0,1:T(8,128)}, u32[]{:S(2)}, u32[]{:S(2)}) collective-permute-start(f32[192,8,128]{2,0,1:T(8,128)} %add.195), channel_id=1, source_target_pairs={{0,1},{1,2},{2,3},{3,4},{4,5},{5,6},{6,7},{7,0},{8,9},{9,10},{10,1... | collective-permute-start | bytes 2359304 | tf_op jit(solution)/shard_map/ppermute | solution.py:16
  580.5 5.3 collective-permute-start.19
  591.5 24.1 %collective-permute-done.19 = bf16[192,1024]{1,0:T(8,128)(2,1)S(1)} collective-permute-done((bf16[192,1024]{1,0:T(8,128)(2,1)}, bf16[192,1024]{1,0:T(8,128)(2,1)S(1)}, u32[]{:S(2)}, u32[]{:S(2)}) %collective-permute-start.19) | collective-permute-done | bytes 393248 | tf_op jit(solution)/shard_map/ppermute | solution.py:22
  633.3 11.1 %multiply_convert_fusion = bf16[192,8,4,128]{3,0,2,1:T(8,128)(2,1)S(1)} fusion(f32[192,8,4,128]{3,0,2,1:T(8,128)} %get-tuple-element.240, f32[192,8,4,128]{3,0,2,1:T(8,128)} %get-tuple-element.239, f32[192,8,4,128]{3,0,2,1:T(8,128)} %get-tuple-element.238, f32[192,8,4,128]{3,0,2,1:T(8,128)} %get-tuple-element.237, ...), kind=kLoop, calls=%fused_computation.215 | loop fusion | flops 7077888 | bytes 26738688 | tf_op jit(solution)/shard_map/convert_element_type | solution.py:130
  (153 shorter events, 222.8 us)
Async XLA Ops:
  7.2 75.1 %all-gather.2.cloned.1.call-start = ((), (), s32[]{:S(2)}) async-start(), calls=%async_computation | async-start | bytes 3538944 | tf_op jit(solution)/shard_map/all_gather | solution.py:63
  7.9 23.7 %collective-permute-start = (s32[192]{0:T(256)}, s32[192]{0:T(256)S(1)}, u32[]{:S(2)}, u32[]{:S(2)}) collective-permute-start(s32[192]{0:T(256)} %param.29), channel_id=1, source_target_pairs={{0,1},{1,2},{2,3},{3,4},{4,5},{5,6},{6,7},{8,9},{9,10},{10,11},{11... | collective-permute-start | bytes 2312 | tf_op jit(solution)/shard_map/ppermute | solution.py:22
  144.1 54.9 %collective-permute-start.29 = (f32[192,8,128]{2,0,1:T(8,128)}, f32[192,8,128]{2,0,1:T(8,128)}, u32[]{:S(2)}, u32[]{:S(2)}) collective-permute-start(f32[192,8,128]{2,0,1:T(8,128)} %get-tuple-element.249), channel_id=1, source_target_pairs={{0,1},{1,2},{2,3},{3,4},{4,5},{5,6},{6,7},{7,0},{8,9},{9,10},{10,1... | collective-permute-start | bytes 2359304 | tf_op jit(solution)/shard_map/ppermute | solution.py:16
  145.3 78.4 %collective-permute-start.21 = (f32[192,8,128]{2,0,1:T(8,128)}, f32[192,8,128]{2,0,1:T(8,128)}, u32[]{:S(2)}, u32[]{:S(2)}) collective-permute-start(f32[192,8,128]{2,0,1:T(8,128)} %get-tuple-element.241), channel_id=1, source_target_pairs={{0,1},{1,2},{2,3},{3,4},{4,5},{5,6},{6,7},{7,0},{8,9},{9,10},{10,1... | collective-permute-start | bytes 2359304 | tf_op jit(solution)/shard_map/ppermute | solution.py:16
  147.1 41.7 %collective-permute-start.1 = (bf16[192,1024]{1,0:T(8,128)(2,1)S(1)}, bf16[192,1024]{1,0:T(8,128)(2,1)}, u32[]{:S(2)}, u32[]{:S(2)}) collective-permute-start(bf16[192,1024]{1,0:T(8,128)(2,1)S(1)} %copy-done.1), channel_id=1, source_target_pairs={{0,1},{1,2},{2,3},{3,4},{4,5},{5,6},{6,7},{8,9},{9,10},{10,11},{11... | collective-permute-start | bytes 1179656 | tf_op jit(solution)/shard_map/ppermute | solution.py:22
  152.0 43.4 %collective-permute-start.2 = (bf16[192,1024]{1,0:T(8,128)(2,1)S(1)}, bf16[192,1024]{1,0:T(8,128)(2,1)}, u32[]{:S(2)}, u32[]{:S(2)}) collective-permute-start(bf16[192,1024]{1,0:T(8,128)(2,1)S(1)} %copy-done.10), channel_id=1, source_target_pairs={{0,1},{1,2},{2,3},{3,4},{4,5},{5,6},{6,7},{8,9},{9,10},{10,11},{11... | collective-permute-start | bytes 1179656 | tf_op jit(solution)/shard_map/ppermute | solution.py:22
  201.4 75.7 %collective-permute-start.30 = (f32[192,8,128]{2,0,1:T(8,128)}, f32[192,8,128]{2,0,1:T(8,128)}, u32[]{:S(2)}, u32[]{:S(2)}) collective-permute-start(f32[192,8,128]{2,0,1:T(8,128)} %add.190), channel_id=1, source_target_pairs={{0,1},{1,2},{2,3},{3,4},{4,5},{5,6},{6,7},{7,0},{8,9},{9,10},{10,1... | collective-permute-start | bytes 2359304 | tf_op jit(solution)/shard_map/ppermute | solution.py:16
  225.8 57.1 %collective-permute-start.22 = (f32[192,8,128]{2,0,1:T(8,128)}, f32[192,8,128]{2,0,1:T(8,128)}, u32[]{:S(2)}, u32[]{:S(2)}) collective-permute-start(f32[192,8,128]{2,0,1:T(8,128)} %add.183), channel_id=1, source_target_pairs={{0,1},{1,2},{2,3},{3,4},{4,5},{5,6},{6,7},{7,0},{8,9},{9,10},{10,1... | collective-permute-start | bytes 2359304 | tf_op jit(solution)/shard_map/ppermute | solution.py:16
  229.3 38.0 %collective-permute-start.4 = (bf16[192,1024]{1,0:T(8,128)(2,1)}, bf16[192,1024]{1,0:T(8,128)(2,1)}, u32[]{:S(2)}, u32[]{:S(2)}) collective-permute-start(bf16[192,1024]{1,0:T(8,128)(2,1)} %collective-permute-done.1), channel_id=1, source_target_pairs={{0,1},{1,2},{2,3},{3,4},{4,5},{5,6},{6,7},{8,9},{9,10},{10,11},{11... | collective-permute-start | bytes 1179656 | tf_op jit(solution)/shard_map/ppermute | solution.py:22
  233.3 40.7 %collective-permute-start.5 = (bf16[192,1024]{1,0:T(8,128)(2,1)}, bf16[192,1024]{1,0:T(8,128)(2,1)}, u32[]{:S(2)}, u32[]{:S(2)}) collective-permute-start(bf16[192,1024]{1,0:T(8,128)(2,1)} %collective-permute-done.2), channel_id=1, source_target_pairs={{0,1},{1,2},{2,3},{3,4},{4,5},{5,6},{6,7},{8,9},{9,10},{10,11},{11... | collective-permute-start | bytes 1179656 | tf_op jit(solution)/shard_map/ppermute | solution.py:22
  279.4 64.0 %collective-permute-start.31 = (f32[192,8,128]{2,0,1:T(8,128)}, f32[192,8,128]{2,0,1:T(8,128)}, u32[]{:S(2)}, u32[]{:S(2)}) collective-permute-start(f32[192,8,128]{2,0,1:T(8,128)} %add.191), channel_id=1, source_target_pairs={{0,1},{1,2},{2,3},{3,4},{4,5},{5,6},{6,7},{7,0},{8,9},{9,10},{10,1... | collective-permute-start | bytes 2359304 | tf_op jit(solution)/shard_map/ppermute | solution.py:16
  285.0 75.9 %collective-permute-start.23 = (f32[192,8,128]{2,0,1:T(8,128)}, f32[192,8,128]{2,0,1:T(8,128)}, u32[]{:S(2)}, u32[]{:S(2)}) collective-permute-start(f32[192,8,128]{2,0,1:T(8,128)} %add.184), channel_id=1, source_target_pairs={{0,1},{1,2},{2,3},{3,4},{4,5},{5,6},{6,7},{7,0},{8,9},{9,10},{10,1... | collective-permute-start | bytes 2359304 | tf_op jit(solution)/shard_map/ppermute | solution.py:16
  308.0 26.7 %collective-permute-start.7 = (bf16[192,1024]{1,0:T(8,128)(2,1)}, bf16[192,1024]{1,0:T(8,128)(2,1)}, u32[]{:S(2)}, u32[]{:S(2)}) collective-permute-start(bf16[192,1024]{1,0:T(8,128)(2,1)} %collective-permute-done.4), channel_id=1, source_target_pairs={{0,1},{1,2},{2,3},{3,4},{4,5},{5,6},{6,7},{8,9},{9,10},{10,11},{11... | collective-permute-start | bytes 1179656 | tf_op jit(solution)/shard_map/ppermute | solution.py:22
  311.1 29.1 %collective-permute-start.8 = (bf16[192,1024]{1,0:T(8,128)(2,1)}, bf16[192,1024]{1,0:T(8,128)(2,1)}, u32[]{:S(2)}, u32[]{:S(2)}) collective-permute-start(bf16[192,1024]{1,0:T(8,128)(2,1)} %collective-permute-done.5), channel_id=1, source_target_pairs={{0,1},{1,2},{2,3},{3,4},{4,5},{5,6},{6,7},{8,9},{9,10},{10,11},{11... | collective-permute-start | bytes 1179656 | tf_op jit(solution)/shard_map/ppermute | solution.py:22
  345.9 66.9 %collective-permute-start.32 = (f32[192,8,128]{2,0,1:T(8,128)}, f32[192,8,128]{2,0,1:T(8,128)}, u32[]{:S(2)}, u32[]{:S(2)}) collective-permute-start(f32[192,8,128]{2,0,1:T(8,128)} %add.192), channel_id=1, source_target_pairs={{0,1},{1,2},{2,3},{3,4},{4,5},{5,6},{6,7},{7,0},{8,9},{9,10},{10,1... | collective-permute-start | bytes 2359304 | tf_op jit(solution)/shard_map/ppermute | solution.py:16
  363.0 59.7 %collective-permute-start.24 = (f32[192,8,128]{2,0,1:T(8,128)}, f32[192,8,128]{2,0,1:T(8,128)}, u32[]{:S(2)}, u32[]{:S(2)}) collective-permute-start(f32[192,8,128]{2,0,1:T(8,128)} %add.185), channel_id=1, source_target_pairs={{0,1},{1,2},{2,3},{3,4},{4,5},{5,6},{6,7},{7,0},{8,9},{9,10},{10,1... | collective-permute-start | bytes 2359304 | tf_op jit(solution)/shard_map/ppermute | solution.py:16
  366.4 38.1 %collective-permute-start.10 = (bf16[192,1024]{1,0:T(8,128)(2,1)}, bf16[192,1024]{1,0:T(8,128)(2,1)}, u32[]{:S(2)}, u32[]{:S(2)}) collective-permute-start(bf16[192,1024]{1,0:T(8,128)(2,1)} %collective-permute-done.7), channel_id=1, source_target_pairs={{0,1},{1,2},{2,3},{3,4},{4,5},{5,6},{6,7},{8,9},{9,10},{10,11},{11... | collective-permute-start | bytes 1179656 | tf_op jit(solution)/shard_map/ppermute | solution.py:22
  388.2 21.0 %collective-permute-start.11 = (bf16[192,1024]{1,0:T(8,128)(2,1)}, bf16[192,1024]{1,0:T(8,128)(2,1)}, u32[]{:S(2)}, u32[]{:S(2)}) collective-permute-start(bf16[192,1024]{1,0:T(8,128)(2,1)} %collective-permute-done.8), channel_id=1, source_target_pairs={{0,1},{1,2},{2,3},{3,4},{4,5},{5,6},{6,7},{8,9},{9,10},{10,11},{11... | collective-permute-start | bytes 1179656 | tf_op jit(solution)/shard_map/ppermute | solution.py:22
  415.1 63.8 %collective-permute-start.33 = (f32[192,8,128]{2,0,1:T(8,128)}, f32[192,8,128]{2,0,1:T(8,128)}, u32[]{:S(2)}, u32[]{:S(2)}) collective-permute-start(f32[192,8,128]{2,0,1:T(8,128)} %add.193), channel_id=1, source_target_pairs={{0,1},{1,2},{2,3},{3,4},{4,5},{5,6},{6,7},{7,0},{8,9},{9,10},{10,1... | collective-permute-start | bytes 2359304 | tf_op jit(solution)/shard_map/ppermute | solution.py:16
  424.8 66.0 %collective-permute-start.25 = (f32[192,8,128]{2,0,1:T(8,128)}, f32[192,8,128]{2,0,1:T(8,128)}, u32[]{:S(2)}, u32[]{:S(2)}) collective-permute-start(f32[192,8,128]{2,0,1:T(8,128)} %add.186), channel_id=1, source_target_pairs={{0,1},{1,2},{2,3},{3,4},{4,5},{5,6},{6,7},{7,0},{8,9},{9,10},{10,1... | collective-permute-start | bytes 2359304 | tf_op jit(solution)/shard_map/ppermute | solution.py:16
  439.8 31.6 %collective-permute-start.13 = (bf16[192,1024]{1,0:T(8,128)(2,1)}, bf16[192,1024]{1,0:T(8,128)(2,1)}, u32[]{:S(2)}, u32[]{:S(2)}) collective-permute-start(bf16[192,1024]{1,0:T(8,128)(2,1)} %collective-permute-done.10), channel_id=1, source_target_pairs={{0,1},{1,2},{2,3},{3,4},{4,5},{5,6},{6,7},{8,9},{9,10},{10,11},{11... | collective-permute-start | bytes 1179656 | tf_op jit(solution)/shard_map/ppermute | solution.py:22
  445.9 29.8 %collective-permute-start.14 = (bf16[192,1024]{1,0:T(8,128)(2,1)}, bf16[192,1024]{1,0:T(8,128)(2,1)}, u32[]{:S(2)}, u32[]{:S(2)}) collective-permute-start(bf16[192,1024]{1,0:T(8,128)(2,1)} %collective-permute-done.11), channel_id=1, source_target_pairs={{0,1},{1,2},{2,3},{3,4},{4,5},{5,6},{6,7},{8,9},{9,10},{10,11},{11... | collective-permute-start | bytes 1179656 | tf_op jit(solution)/shard_map/ppermute | solution.py:22
  481.3 76.3 %collective-permute-start.34 = (f32[192,8,128]{2,0,1:T(8,128)}, f32[192,8,128]{2,0,1:T(8,128)}, u32[]{:S(2)}, u32[]{:S(2)}) collective-permute-start(f32[192,8,128]{2,0,1:T(8,128)} %add.194), channel_id=1, source_target_pairs={{0,1},{1,2},{2,3},{3,4},{4,5},{5,6},{6,7},{7,0},{8,9},{9,10},{10,1... | collective-permute-start | bytes 2359304 | tf_op jit(solution)/shard_map/ppermute | solution.py:16
  493.0 82.0 %collective-permute-start.26 = (f32[192,8,128]{2,0,1:T(8,128)}, f32[192,8,128]{2,0,1:T(8,128)}, u32[]{:S(2)}, u32[]{:S(2)}) collective-permute-start(f32[192,8,128]{2,0,1:T(8,128)} %add.187), channel_id=1, source_target_pairs={{0,1},{1,2},{2,3},{3,4},{4,5},{5,6},{6,7},{7,0},{8,9},{9,10},{10,1... | collective-permute-start | bytes 2359304 | tf_op jit(solution)/shard_map/ppermute | solution.py:16
  504.4 49.9 %collective-permute-start.16 = (bf16[192,1024]{1,0:T(8,128)(2,1)}, bf16[192,1024]{1,0:T(8,128)(2,1)}, u32[]{:S(2)}, u32[]{:S(2)}) collective-permute-start(bf16[192,1024]{1,0:T(8,128)(2,1)} %collective-permute-done.13), channel_id=1, source_target_pairs={{0,1},{1,2},{2,3},{3,4},{4,5},{5,6},{6,7},{8,9},{9,10},{10,11},{11... | collective-permute-start | bytes 1179656 | tf_op jit(solution)/shard_map/ppermute | solution.py:22
  522.1 32.2 %collective-permute-start.17 = (bf16[192,1024]{1,0:T(8,128)(2,1)}, bf16[192,1024]{1,0:T(8,128)(2,1)}, u32[]{:S(2)}, u32[]{:S(2)}) collective-permute-start(bf16[192,1024]{1,0:T(8,128)(2,1)} %collective-permute-done.14), channel_id=1, source_target_pairs={{0,1},{1,2},{2,3},{3,4},{4,5},{5,6},{6,7},{8,9},{9,10},{10,11},{11... | collective-permute-start | bytes 1179656 | tf_op jit(solution)/shard_map/ppermute | solution.py:22
  560.0 62.2 %collective-permute-start.35 = (f32[192,8,128]{2,0,1:T(8,128)}, f32[192,8,128]{2,0,1:T(8,128)}, u32[]{:S(2)}, u32[]{:S(2)}) collective-permute-start(f32[192,8,128]{2,0,1:T(8,128)} %add.195), channel_id=1, source_target_pairs={{0,1},{1,2},{2,3},{3,4},{4,5},{5,6},{6,7},{7,0},{8,9},{9,10},{10,1... | collective-permute-start | bytes 2359304 | tf_op jit(solution)/shard_map/ppermute | solution.py:16
  577.1 50.4 %collective-permute-start.27 = (f32[192,8,128]{2,0,1:T(8,128)}, f32[192,8,128]{2,0,1:T(8,128)}, u32[]{:S(2)}, u32[]{:S(2)}) collective-permute-start(f32[192,8,128]{2,0,1:T(8,128)} %add.188), channel_id=1, source_target_pairs={{0,1},{1,2},{2,3},{3,4},{4,5},{5,6},{6,7},{7,0},{8,9},{9,10},{10,1... | collective-permute-start | bytes 2359304 | tf_op jit(solution)/shard_map/ppermute | solution.py:16
  580.5 35.1 %collective-permute-start.19 = (bf16[192,1024]{1,0:T(8,128)(2,1)}, bf16[192,1024]{1,0:T(8,128)(2,1)S(1)}, u32[]{:S(2)}, u32[]{:S(2)}) collective-permute-start(bf16[192,1024]{1,0:T(8,128)(2,1)} %collective-permute-done.16), channel_id=1, source_target_pairs={{0,1},{1,2},{2,3},{3,4},{4,5},{5,6},{6,7},{8,9},{9,10},{10,11},{11... | collective-permute-start | bytes 1179656 | tf_op jit(solution)/shard_map/ppermute | solution.py:22
  585.8 34.0 %collective-permute-start.20 = (bf16[192,1024]{1,0:T(8,128)(2,1)}, bf16[192,1024]{1,0:T(8,128)(2,1)S(1)}, u32[]{:S(2)}, u32[]{:S(2)}) collective-permute-start(bf16[192,1024]{1,0:T(8,128)(2,1)} %collective-permute-done.17), channel_id=1, source_target_pairs={{0,1},{1,2},{2,3},{3,4},{4,5},{5,6},{6,7},{8,9},{9,10},{10,11},{11... | collective-permute-start | bytes 1179656 | tf_op jit(solution)/shard_map/ppermute | solution.py:22
  624.1 26.5 %collective-permute-start.36 = (bf16[192,8,128]{2,0,1:T(8,128)(2,1)}, bf16[192,8,128]{2,0,1:T(8,128)(2,1)S(1)}, u32[]{:S(2)}, u32[]{:S(2)}) collective-permute-start(bf16[192,8,128]{2,0,1:T(8,128)(2,1)} %add.196), channel_id=1, source_target_pairs={{0,1},{1,2},{2,3},{3,4},{4,5},{5,6},{6,7},{7,0},{8,9},{9,10},{10,1... | collective-permute-start | bytes 1179656 | tf_op jit(solution)/shard_map/ppermute | solution.py:16
  629.6 21.8 %collective-permute-start.28 = (f32[192,8,128]{2,0,1:T(8,128)}, f32[192,8,128]{2,0,1:T(8,128)S(1)}, u32[]{:S(2)}, u32[]{:S(2)}) collective-permute-start(f32[192,8,128]{2,0,1:T(8,128)} %add.189), channel_id=1, source_target_pairs={{0,1},{1,2},{2,3},{3,4},{4,5},{5,6},{6,7},{7,0},{8,9},{9,10},{10,1... | collective-permute-start | bytes 2359304 | tf_op jit(solution)/shard_map/ppermute | solution.py:16
  (19 other events, 513.8 us)
Sparse Core Ops, SparseCore 0:
  9.6 72.5 all-gather.1
where the time goes:
time: 669 us; the launch traced here: 660 us
  starting transfers between devices  290 us (43%)
  waiting for transfers between devices  177 us (26%)
  other arithmetic  73.8 us (11%)
  local copies, waits for them, and re-layouts  45.8 us (7%)
  matrix products  36.9 us (6%)
  between operations  21.4 us (3%)
  blocking collectives  11.8 us (2%)
    ppermute x21, waiting for transfers between devices, from_behind_2(): return lax.ppermute(block, axis, route)  163 us
    ppermute x21, starting transfers between devices, from_behind_2(): return lax.ppermute(block, axis, route)  148 us
    ppermute x16, starting transfers between devices, from_behind(): return lax.ppermute(value, axis, pairs)  143 us
    dot_general x2, matrix products, key_scores(): jnp.einsum('qhgd,khd->hgqk', head_queries, rows_of_keys, preferred_elemen...  22.2 us
    another operation x22, local copies, waits for them, and re-layouts  20.8 us
    reduce_sum x1, other arithmetic, update(): jnp.sum(jnp.where(allowed, jnp.exp(masked - new_max[..., None]), 0.0), ax...  17.3 us
    add x7, other arithmetic, local(): value_gradient_total + value_part  16.1 us
    add x7, other arithmetic, local(): key_gradient_total + key_part  14.8 us
  transfers between devices with their start and end apart: 38, of which 17 were waited for; matrix products, arithmetic and copies ran while one was open for 14% of the time, Pallas kernels for 0%

commit v1 on v0

v1 whole, which is shorter than its diff:
```python
import math

import jax
import jax.numpy as jnp
from jax import lax
from jax.experimental import pallas as pl
from jax.experimental.pallas import tpu as pltpu
from jax.sharding import PartitionSpec as P

QUERY_HEADS = 32
KEY_VALUE_HEADS = 8
HEAD_WIDTH = 128
GROUP = QUERY_HEADS // KEY_VALUE_HEADS
DOCS = 8
TOK = 192
BLOCKS = 8
MOST_BLOCKS = 5
PAIR = 2 * TOK
Q_AT = 0
G_AT = GROUP * TOK
K_AT = 2 * GROUP * TOK
V_AT = K_AT + TOK
X_AT = V_AT + TOK
SEND_ROWS = X_AT + 16
BACK_ROWS = (GROUP + 2) * TOK
NT = (((1,), (1,)), ((), ()))
TN = (((0,), (0,)), ((), ()))
NN = (((1,), (0,)), ((), ()))


def dot(a, b, dims):
    return lax.dot_general(a, b, dims, preferred_element_type=jnp.float32)


def rows_of(flat):
    return jnp.concatenate(
        [flat[:, t * 128 : (t + 1) * 128] for t in range(flat.shape[1] // 128)], axis=0
    )


def pack_kernel(q_ref, k_ref, v_ref, o_ref, g_ref, doc_ref, out_ref):
    product = []
    for h in range(GROUP):
        cols = slice(h * HEAD_WIDTH, (h + 1) * HEAD_WIDTH)
        g = g_ref[:, cols]
        out_ref[0, Q_AT + h * TOK : Q_AT + (h + 1) * TOK, :] = q_ref[:, cols]
        out_ref[0, G_AT + h * TOK : G_AT + (h + 1) * TOK, :] = g
        product.append(g.astype(jnp.float32) * o_ref[:, cols].astype(jnp.float32))
    out_ref[0, K_AT : K_AT + TOK, :] = k_ref[...]
    out_ref[0, V_AT : V_AT + TOK, :] = v_ref[...]
    delta = jnp.sum(jnp.concatenate(product, axis=0).T, axis=0, keepdims=True)
    delta = rows_of(delta)
    high = delta.astype(jnp.bfloat16).astype(jnp.float32)
    extra = jnp.concatenate(
        [high, delta - high, doc_ref[...], jnp.zeros((1, 128), jnp.float32)], axis=0
    )
    out_ref[0, X_AT : X_AT + 16, :] = extra.astype(jnp.bfloat16)


def attention_kernel(pay_ref, out_ref, extra_ref, start_ref, first_ref, dk_ref, dv_ref):
    scale = 1.0 / math.sqrt(HEAD_WIDTH)
    to_exp2 = scale * math.log2(math.e)
    dk_ref[...] = jnp.zeros_like(dk_ref)
    dv_ref[...] = jnp.zeros_like(dv_ref)
    for b in range(BLOCKS):
        extra_ref[b] = pay_ref[b, X_AT : X_AT + 16, :].astype(jnp.float32)
    docs = jnp.concatenate([extra_ref[b, 12:15, :] for b in range(BLOCKS)], axis=0)
    starts = jnp.zeros_like(docs)
    for d in range(1, DOCS):
        before = 0.5 * jnp.sum(jnp.where(docs < d, 1.0, 0.0), keepdims=True)
        starts = jnp.where(docs == d, before, starts)
    for b in range(BLOCKS):
        own = starts[3 * b : 3 * b + 3]
        start_ref[b] = jnp.concatenate([own, own, own[:2]], axis=0)
        first_ref[b] = jnp.min(own).astype(jnp.int32)

    def query_block(i, carry):
        first_block = first_ref[i] // TOK
        first_row = start_ref[i]
        start = jnp.concatenate([first_row[t : t + 1] for t in range(3)], axis=1).astype(jnp.int32)
        lane = lax.broadcasted_iota(jnp.int32, (1, PAIR), 1)
        query_pos = jnp.where(lane >= TOK, lane - TOK, lane) + i * TOK
        delta6 = extra_ref[i, 0:6, :] + extra_ref[i, 6:12, :]

        def with_blocks(count):
            low = i - count + 1
            rows = count * TOK
            keys = pay_ref[pl.ds(low, count), K_AT : K_AT + TOK, :].reshape(rows, HEAD_WIDTH)
            values = pay_ref[pl.ds(low, count), V_AT : V_AT + TOK, :].reshape(rows, HEAD_WIDTH)
            key_pos = lax.broadcasted_iota(jnp.int32, (rows, PAIR), 0) + low * TOK
            allowed = (key_pos >= start) & (key_pos <= query_pos)
            dk = jnp.zeros((rows, HEAD_WIDTH), jnp.float32)
            dv = jnp.zeros((rows, HEAD_WIDTH), jnp.float32)
            for pair in range(GROUP // 2):
                q = pay_ref[i, Q_AT + pair * PAIR : Q_AT + (pair + 1) * PAIR, :]
                g = pay_ref[i, G_AT + pair * PAIR : G_AT + (pair + 1) * PAIR, :]
                delta = jnp.concatenate(
                    [delta6[3 * pair + t : 3 * pair + t + 1] for t in range(3)], axis=1
                )
                scores = jnp.where(allowed, dot(keys, q, NT), -1e30)
                top = jnp.max(scores, axis=0, keepdims=True)
                weights = jnp.exp2(scores * to_exp2 - top * to_exp2)
                total = jnp.sum(weights, axis=0, keepdims=True)
                probs = weights * (1.0 / total)
                dv = dv + dot(probs.astype(jnp.bfloat16), g, NN)
                prob_grad = dot(values, g, NT)
                score_grad = (probs * (prob_grad - delta)).astype(jnp.bfloat16)
                dk = dk + dot(score_grad, q, NN)
                dq = dot(score_grad, keys, TN) * scale
                out_ref[i, pair * PAIR : (pair + 1) * PAIR, :] = dq.astype(jnp.bfloat16)
            dk_ref[pl.ds(low, count)] += dk.reshape(count, TOK, HEAD_WIDTH)
            dv_ref[pl.ds(low, count)] += dv.reshape(count, TOK, HEAD_WIDTH)

        for count in range(1, MOST_BLOCKS + 1):
            pl.when(i - first_block + 1 == count)(lambda count=count: with_blocks(count))
        return carry

    lax.fori_loop(0, BLOCKS, query_block, 0)
    at = GROUP * TOK
    out_ref[:, at : at + TOK, :] = (dk_ref[...] * scale).astype(jnp.bfloat16)
    out_ref[:, at + TOK : at + 2 * TOK, :] = dv_ref[...].astype(jnp.bfloat16)


def unpack_kernel(back_ref, dq_ref, dk_ref, dv_ref):
    for h in range(GROUP):
        dq_ref[:, h * HEAD_WIDTH : (h + 1) * HEAD_WIDTH] = back_ref[0, h * TOK : (h + 1) * TOK, :]
    at = GROUP * TOK
    dk_ref[...] = back_ref[0, at : at + TOK, :]
    dv_ref[...] = back_ref[0, at + TOK : at + 2 * TOK, :]


def local(queries, keys, values, outputs, output_gradient, doc_ids):
    wide = pl.BlockSpec((TOK, GROUP * HEAD_WIDTH), lambda g: (0, g))
    narrow = pl.BlockSpec((TOK, HEAD_WIDTH), lambda g: (0, g))
    docs = jnp.tile(doc_ids, 2).reshape(3, 128).astype(jnp.float32)
    packed = pl.pallas_call(
        pack_kernel,
        grid=(KEY_VALUE_HEADS,),
        in_specs=[wide, narrow, narrow, wide, wide, pl.BlockSpec((3, 128), lambda g: (0, 0))],
        out_specs=pl.BlockSpec((1, SEND_ROWS, 128), lambda g: (g, 0, 0)),
        out_shape=jax.ShapeDtypeStruct((KEY_VALUE_HEADS, SEND_ROWS, 128), jnp.bfloat16),
        compiler_params=pltpu.CompilerParams(vmem_limit_bytes=32 * 2**20),
        name="pack",
    )(queries, keys, values, outputs, output_gradient, docs)
    payload = lax.all_to_all(packed, "blk", 0, 0, tiled=True)
    result = pl.pallas_call(
        attention_kernel,
        out_shape=jax.ShapeDtypeStruct((BLOCKS, BACK_ROWS, 128), jnp.bfloat16),
        scratch_shapes=[
            pltpu.VMEM((BLOCKS, 16, 128), jnp.float32),
            pltpu.VMEM((BLOCKS, 8, 128), jnp.float32),
            pltpu.SMEM((BLOCKS,), jnp.int32),
            pltpu.VMEM((BLOCKS, TOK, HEAD_WIDTH), jnp.float32),
            pltpu.VMEM((BLOCKS, TOK, HEAD_WIDTH), jnp.float32),
        ],
        compiler_params=pltpu.CompilerParams(vmem_limit_bytes=48 * 2**20),
        name="attention",
    )(payload)
    back = lax.all_to_all(result, "blk", 0, 0, tiled=True)
    return pl.pallas_call(
        unpack_kernel,
        grid=(KEY_VALUE_HEADS,),
        in_specs=[pl.BlockSpec((1, BACK_ROWS, 128), lambda g: (g, 0, 0))],
        out_specs=[wide, narrow, narrow],
        out_shape=[
            jax.ShapeDtypeStruct(queries.shape, jnp.bfloat16),
            jax.ShapeDtypeStruct(keys.shape, jnp.bfloat16),
            jax.ShapeDtypeStruct(values.shape, jnp.bfloat16),
        ],
        compiler_params=pltpu.CompilerParams(vmem_limit_bytes=32 * 2**20),
        name="unpack",
    )(back)


def solution(mesh):
    rows = P(("dp", "blk"), None)
    return jax.shard_map(
        local,
        mesh=mesh,
        in_specs=(rows, rows, rows, rows, rows, P(("dp", "blk"))),
        out_specs=(rows, rows, rows),
        check_vma=False,
    )
```

time: 669 us -> 116 us (0.17); the launches traced: 660 us -> 115 us
  starting transfers between devices: 290 us -> 0 us
  waiting for transfers between devices: 177 us -> 0 us
  other arithmetic: 73.8 us -> 0.68 us
  blocking collectives: 11.8 us -> 83.9 us
  local copies, waits for them, and re-layouts: 45.8 us -> 6.3 us
  matrix products: 36.9 us -> 0 us
  Pallas kernels: 0 us -> 23.8 us
  between operations: 21.4 us -> 0.65 us
    ppermute x37 -> x0, starting transfers between devices: 290 us -> none  [the longest x21 148 us: from_behind_2(): return lax.ppermute(block, axis, route)]
    ppermute x37 -> x0, waiting for transfers between devices: 163 us -> none  [the longest x21 163 us: from_behind_2(): return lax.ppermute(block, axis, route)]
    all_to_all x0 -> x2, blocking collectives: none -> 83.9 us  [the longest x1 53.3 us: local(): payload = lax.all_to_all(packed, 'blk', 0, 0, tiled=True)]
    dot_general x6 -> x0, matrix products: 36.9 us -> none  [the longest x2 22.2 us: key_scores(): jnp.einsum('qhgd,khd->hgqk', head_queries, rows_of_keys, preferred_elemen...]
    add x20 -> x0, other arithmetic: 31.8 us -> none  [the longest x7 16.1 us: local(): value_gradient_total + value_part]
    pallas_call x0 -> x3, Pallas kernels: none -> 23.8 us  [the longest x1 18.2 us: local(): pl.pallas_call(attention_kernel, out_shape=jax.ShapeDtypeStruct((BLOCKS,...]
    reduce_sum x2 -> x0, other arithmetic: 20.9 us -> none  [the longest x1 17.3 us: update(): jnp.sum(jnp.where(allowed, jnp.exp(masked - new_max[..., None]), 0.0), ax...]
    another operation x22 -> x1, local copies, waits for them, and re-layouts: 20.8 us -> 0.01 us  [local(): docs = jnp.tile(doc_ids, 2).reshape(3, 128).astype(jnp.float32)]
  transfers between devices with their start and end apart: 38 -> 0, of which waited for: 17 -> 0; matrix products, arithmetic and copies ran while one was open for 14% -> 0% of each run, Pallas kernels for 0% -> 0%
where the time goes in v1:
time: 116 us; the launch traced here: 115 us
  blocking collectives  83.9 us (72%)
  Pallas kernels  23.8 us (21%)
  local copies, waits for them, and re-layouts  6.3 us (5%)
    all_to_all x1, blocking collectives, local(): payload = lax.all_to_all(packed, 'blk', 0, 0, tiled=True)  53.3 us
    all_to_all x1, blocking collectives, local(): back = lax.all_to_all(result, 'blk', 0, 0, tiled=True)  30.6 us
    pallas_call x1, Pallas kernels, local(): pl.pallas_call(attention_kernel, out_shape=jax.ShapeDtypeStruct((BLOCKS,...  18.2 us
    unnamed x10, local copies, waits for them, and re-layouts  6.21 us
    pallas_call x1, Pallas kernels, local(): pl.pallas_call(unpack_kernel, grid=(KEY_VALUE_HEADS,), in_specs=[pl.Block...  3.05 us
    pallas_call x1, Pallas kernels, local(): pl.pallas_call(pack_kernel, grid=(KEY_VALUE_HEADS,), in_specs=[wide, narr...  2.51 us

profile of v1, /device:TPU:0, one launch (start us, length us, event | category | flops | bytes accessed | tf_op | source)
XLA Modules:
  0.0 115.3 jit_solution(11812312757302046945)
XLA Ops:
  0.6 0.7 convert_element_type.5
  1.3 0.1 convert_element_type.6.doc_ref
  1.4 0.0 copy-start
  1.4 1.4 %copy-done = bf16[192,4096]{1,0:T(8,128)(2,1)S(1)} copy-done((bf16[192,4096]{1,0:T(8,128)(2,1)S(1)}, bf16[192,4096]{1,0:T(8,128)(2,1)}, u32[]{:S(2)}) %copy-start) | copy-done | bytes 1572888
  2.8 0.0 copy-start.1
  2.8 1.4 %copy-done.1 = bf16[192,4096]{1,0:T(8,128)(2,1)S(1)} copy-done((bf16[192,4096]{1,0:T(8,128)(2,1)S(1)}, bf16[192,4096]{1,0:T(8,128)(2,1)}, u32[]{:S(2)}) %copy-start.1) | copy-done | bytes 1572888
  4.2 0.0 copy-start.2
  4.2 1.4 %copy-done.2 = bf16[192,4096]{1,0:T(8,128)(2,1)S(1)} copy-done((bf16[192,4096]{1,0:T(8,128)(2,1)S(1)}, bf16[192,4096]{1,0:T(8,128)(2,1)}, u32[]{:S(2)}) %copy-start.2) | copy-done | bytes 1572888
  5.6 0.0 copy-start.3
  5.6 1.0 copy-done.3
  6.6 0.0 copy-start.4
  6.6 1.0 copy-done.4
  7.6 2.5 %pack.1 = bf16[8,1936,128]{2,1,0:T(8,128)(2,1)S(1)} custom-call(bf16[192,4096]{1,0:T(8,128)(2,1)S(1)} %copy-done, bf16[192,1024]{1,0:T(8,128)(2,1)S(1)} %copy-done.3, bf16[192,1024]{1,0:T(8,128)(2,1)S(1)} %copy-done.4, bf16[192,4096]{1,0:T(8,128)(2,1)S(1)} %copy-done.1, bf16[192,4096]{1,0:T(8,128)(2,1)S(1)} %copy-done.2, ...), custom_call_target="tpu_custom_call" | custom-call | tf_op jit(solution)/shard_map/pack/pallas_call | solution.py:136
  10.1 53.3 %all_to_all.10.pay_ref = bf16[8,1936,128]{2,1,0:T(8,128)(2,1)} all-to-all(bf16[8,1936,128]{2,1,0:T(8,128)(2,1)S(1)} %pack.1), channel_id=1, replica_groups=mesh['dp'=16,'blk'=8] {'blk'}, dimensions={0} | all-to-all | bytes 7929856 | tf_op jit(solution)/shard_map/all_to_all | solution.py:145
  63.5 18.2 %attention.1 = bf16[8,1152,128]{2,1,0:T(8,128)(2,1)S(1)} custom-call(bf16[8,1936,128]{2,1,0:T(8,128)(2,1)} %all_to_all.10.pay_ref), custom_call_target="tpu_custom_call" | custom-call | tf_op jit(solution)/shard_map/attention/pallas_call | solution.py:146
  81.7 30.6 %all_to_all.11.back_ref = bf16[8,1152,128]{2,1,0:T(8,128)(2,1)S(1)} all-to-all(bf16[8,1152,128]{2,1,0:T(8,128)(2,1)S(1)} %attention.1), channel_id=1, replica_groups=mesh['dp'=16,'blk'=8] {'blk'}, dimensions={0} | all-to-all | bytes 4718592 | tf_op jit(solution)/shard_map/all_to_all | solution.py:159
  112.3 3.1 %unpack.1 = (bf16[192,4096]{1,0:T(8,128)(2,1)}, bf16[192,1024]{1,0:T(8,128)(2,1)}, bf16[192,1024]{1,0:T(8,128)(2,1)}) custom-call(bf16[8,1152,128]{2,1,0:T(8,128)(2,1)S(1)} %all_to_all.11.back_ref), custom_call_target="tpu_custom_call" | custom-call | tf_op jit(solution)/shard_map/unpack/pallas_call | solution.py:160
  (1 shorter events, 0.0 us)
Async XLA Ops:
  1.4 1.4 %copy-start = (bf16[192,4096]{1,0:T(8,128)(2,1)S(1)}, bf16[192,4096]{1,0:T(8,128)(2,1)}, u32[]{:S(2)}) copy-start(bf16[192,4096]{1,0:T(8,128)(2,1)} %q_ref.1) | copy-start | bytes 4718596
  2.8 1.4 %copy-start.1 = (bf16[192,4096]{1,0:T(8,128)(2,1)S(1)}, bf16[192,4096]{1,0:T(8,128)(2,1)}, u32[]{:S(2)}) copy-start(bf16[192,4096]{1,0:T(8,128)(2,1)} %o_ref.1) | copy-start | bytes 4718596
  4.2 1.4 %copy-start.2 = (bf16[192,4096]{1,0:T(8,128)(2,1)S(1)}, bf16[192,4096]{1,0:T(8,128)(2,1)}, u32[]{:S(2)}) copy-start(bf16[192,4096]{1,0:T(8,128)(2,1)} %g_ref.1) | copy-start | bytes 4718596
  5.6 1.0 copy-start.3
  6.6 1.0 copy-start.4

commit v2 on v1

v2 whole, which is shorter than its diff:
```python
import math

import jax
import jax.numpy as jnp
from jax import lax
from jax.experimental import pallas as pl
from jax.experimental.pallas import tpu as pltpu
from jax.sharding import PartitionSpec as P

QUERY_HEADS = 32
KEY_VALUE_HEADS = 8
HEAD_WIDTH = 128
GROUP = QUERY_HEADS // KEY_VALUE_HEADS
DOCS = 8
TOK = 192
BLOCKS = 8
MOST_BLOCKS = 5
WIDE = GROUP * TOK
Q_AT = 0
G_AT = GROUP * TOK
K_AT = 2 * GROUP * TOK
V_AT = K_AT + TOK
X_AT = V_AT + TOK
SEND_ROWS = X_AT + 16
BACK_ROWS = (GROUP + 2) * TOK
NT = (((1,), (1,)), ((), ()))
TN = (((0,), (0,)), ((), ()))
NN = (((1,), (0,)), ((), ()))


def dot(a, b, dims):
    return lax.dot_general(a, b, dims, preferred_element_type=jnp.float32)


def pack_kernel(q_ref, k_ref, v_ref, o_ref, g_ref, doc_ref, out_ref, send, o_buf, g_sem, kv_sem, sem):
    def column(ref, at):
        return ref.at[:, at * HEAD_WIDTH : (at + 1) * HEAD_WIDTH]

    arrivals = []
    for group in range(KEY_VALUE_HEADS):
        copies = []
        for h in range(GROUP):
            head = group * GROUP + h
            rows = pl.ds(G_AT + h * TOK, TOK)
            own = pl.ds(h * TOK, TOK)
            copies += [
                pltpu.make_async_copy(column(g_ref, head), send.at[group, rows], g_sem.at[0, head]),
                pltpu.make_async_copy(column(o_ref, head), o_buf.at[group, own], g_sem.at[1, head]),
                pltpu.make_async_copy(column(q_ref, head), send.at[group, own], g_sem.at[2, head]),
            ]
        for n, (ref, at) in enumerate(((k_ref, K_AT), (v_ref, V_AT))):
            rows = pl.ds(at, TOK)
            copies.append(
                pltpu.make_async_copy(column(ref, group), send.at[group, rows], kv_sem.at[n, group])
            )
        for copy in copies:
            copy.start()
        arrivals.append(copies)
    doc = doc_ref[...].astype(jnp.float32)
    doc = jnp.concatenate([doc, doc], axis=1)
    tail = jnp.concatenate([doc[:, t * 128 : (t + 1) * 128] for t in range(3)], axis=0)
    tail = jnp.concatenate([tail, jnp.zeros((1, 128), jnp.float32)], axis=0)
    departures = []
    for group in range(KEY_VALUE_HEADS):
        for copy in arrivals[group]:
            copy.wait()
        g = send[group, G_AT : G_AT + WIDE, :].astype(jnp.float32)
        product = g * o_buf[group].astype(jnp.float32)
        delta = jnp.sum(product.T, axis=0, keepdims=True)
        delta = jnp.concatenate([delta[:, t * 128 : (t + 1) * 128] for t in range(6)], axis=0)
        high = delta.astype(jnp.bfloat16).astype(jnp.float32)
        extra = jnp.concatenate([high, delta - high, tail], axis=0)
        send[group, X_AT : X_AT + 16, :] = extra.astype(jnp.bfloat16)
        departures.append(pltpu.make_async_copy(send.at[group], out_ref.at[group], sem.at[group]))
        departures[group].start()
    for copy in departures:
        copy.wait()


def attention_kernel(pay_ref, out_ref, extra_ref, start_ref, first_ref, dk_ref, dv_ref):
    scale = 1.0 / math.sqrt(HEAD_WIDTH)
    to_exp2 = scale * math.log2(math.e)
    dk_ref[...] = jnp.zeros_like(dk_ref)
    dv_ref[...] = jnp.zeros_like(dv_ref)
    for b in range(BLOCKS):
        extra_ref[b] = pay_ref[b, X_AT : X_AT + 16, :].astype(jnp.float32)
    docs = jnp.concatenate([extra_ref[b, 12:15, :] for b in range(BLOCKS)], axis=0)
    starts = jnp.zeros_like(docs)
    for d in range(1, DOCS):
        before = 0.5 * jnp.sum(jnp.where(docs < d, 1.0, 0.0), keepdims=True)
        starts = jnp.where(docs == d, before, starts)
    for b in range(BLOCKS):
        own = starts[3 * b : 3 * b + 3]
        start_ref[b] = jnp.concatenate([own, own, own[:2]], axis=0)
        first_ref[b] = jnp.min(own).astype(jnp.int32)

    def query_block(i, carry):
        first_block = first_ref[i] // TOK
        first_row = start_ref[i]
        start = jnp.concatenate([first_row[t : t + 1] for t in range(6)], axis=1).astype(jnp.int32)
        delta6 = extra_ref[i, 0:6, :] + extra_ref[i, 6:12, :]
        delta = jnp.concatenate([delta6[t : t + 1] for t in range(6)], axis=1)
        lane = lax.broadcasted_iota(jnp.int32, (1, WIDE), 1)
        own_row = lane
        for h in range(1, GROUP):
            own_row = jnp.where(lane >= h * TOK, lane - h * TOK, own_row)

        def with_blocks(count):
            low = i - count + 1
            rows = count * TOK
            keys = pay_ref[pl.ds(low, count), K_AT : K_AT + TOK, :].reshape(rows, HEAD_WIDTH)
            values = pay_ref[pl.ds(low, count), V_AT : V_AT + TOK, :].reshape(rows, HEAD_WIDTH)
            q = pay_ref[i, Q_AT : Q_AT + WIDE, :]
            g = pay_ref[i, G_AT : G_AT + WIDE, :]
            key_row = lax.broadcasted_iota(jnp.int32, (rows, WIDE), 0)
            scores = jnp.where(key_row >= start - low * TOK, dot(keys, q, NT), -1e30)
            edge = jnp.where(key_row[:TOK] <= own_row, scores[rows - TOK :], -1e30)
            scores = jnp.concatenate([scores[: rows - TOK], edge], axis=0) if count > 1 else edge
            top = jnp.max(scores, axis=0, keepdims=True)
            weights = jnp.exp2(scores * to_exp2 - top * to_exp2)
            total = jnp.sum(weights, axis=0, keepdims=True)
            probs = weights * (1.0 / total)
            dv = dot(probs.astype(jnp.bfloat16), g, NN)
            prob_grad = dot(values, g, NT)
            score_grad = (probs * (prob_grad - delta)).astype(jnp.bfloat16)
            dk = dot(score_grad, q, NN)
            dq = dot(keys, score_grad, TN).T
            out_ref[i, 0:WIDE, :] = (dq * scale).astype(jnp.bfloat16)
            dk_ref[pl.ds(low, count)] += dk.reshape(count, TOK, HEAD_WIDTH)
            dv_ref[pl.ds(low, count)] += dv.reshape(count, TOK, HEAD_WIDTH)

        for count in range(1, MOST_BLOCKS + 1):
            pl.when(i - first_block + 1 == count)(lambda count=count: with_blocks(count))
        return carry

    lax.fori_loop(0, BLOCKS, query_block, 0)
    at = GROUP * TOK
    out_ref[:, at : at + TOK, :] = (dk_ref[...] * scale).astype(jnp.bfloat16)
    out_ref[:, at + TOK : at + 2 * TOK, :] = dv_ref[...].astype(jnp.bfloat16)


def unpack_kernel(back_ref, dq_ref, dk_ref, dv_ref, sem):
    copies = []

    def send(group, at, ref, column):
        copies.append(
            pltpu.make_async_copy(
                back_ref.at[group, pl.ds(at, TOK)],
                ref.at[:, column * HEAD_WIDTH : (column + 1) * HEAD_WIDTH],
                sem.at[len(copies)],
            )
        )

    for group in range(KEY_VALUE_HEADS):
        for h in range(GROUP):
            send(group, h * TOK, dq_ref, group * GROUP + h)
        send(group, GROUP * TOK, dk_ref, group)
        send(group, (GROUP + 1) * TOK, dv_ref, group)
    for copy in copies:
        copy.start()
    for copy in copies:
        copy.wait()


def local(queries, keys, values, outputs, output_gradient, doc_ids):
    hbm = pl.BlockSpec(memory_space=pltpu.HBM)
    vmem = pl.BlockSpec(memory_space=pltpu.VMEM)
    packed = pl.pallas_call(
        pack_kernel,
        in_specs=[hbm] * 5 + [vmem],
        out_specs=hbm,
        out_shape=jax.ShapeDtypeStruct((KEY_VALUE_HEADS, SEND_ROWS, 128), jnp.bfloat16),
        scratch_shapes=[
            pltpu.VMEM((KEY_VALUE_HEADS, SEND_ROWS, 128), jnp.bfloat16),
            pltpu.VMEM((KEY_VALUE_HEADS, WIDE, HEAD_WIDTH), jnp.bfloat16),
            pltpu.SemaphoreType.DMA((3, QUERY_HEADS)),
            pltpu.SemaphoreType.DMA((2, KEY_VALUE_HEADS)),
            pltpu.SemaphoreType.DMA((KEY_VALUE_HEADS,)),
        ],
        compiler_params=pltpu.CompilerParams(vmem_limit_bytes=62 * 2**20),
        name="pack",
    )(queries, keys, values, outputs, output_gradient, doc_ids.reshape(1, TOK))
    payload = lax.all_to_all(packed, "blk", 0, 0, tiled=True)
    result = pl.pallas_call(
        attention_kernel,
        out_shape=jax.ShapeDtypeStruct((BLOCKS, BACK_ROWS, 128), jnp.bfloat16),
        scratch_shapes=[
            pltpu.VMEM((BLOCKS, 16, 128), jnp.float32),
            pltpu.VMEM((BLOCKS, 8, 128), jnp.float32),
            pltpu.SMEM((BLOCKS,), jnp.int32),
            pltpu.VMEM((BLOCKS, TOK, HEAD_WIDTH), jnp.float32),
            pltpu.VMEM((BLOCKS, TOK, HEAD_WIDTH), jnp.float32),
        ],
        compiler_params=pltpu.CompilerParams(vmem_limit_bytes=32 * 2**20),
        name="attention",
    )(payload)
    back = lax.all_to_all(result, "blk", 0, 0, tiled=True)
    return pl.pallas_call(
        unpack_kernel,
        in_specs=[pl.BlockSpec(memory_space=pl.ANY)],
        out_specs=[hbm] * 3,
        out_shape=[
            jax.ShapeDtypeStruct(queries.shape, jnp.bfloat16),
            jax.ShapeDtypeStruct(keys.shape, jnp.bfloat16),
            jax.ShapeDtypeStruct(values.shape, jnp.bfloat16),
        ],
        scratch_shapes=[pltpu.SemaphoreType.DMA((QUERY_HEADS + 2 * KEY_VALUE_HEADS,))],
        compiler_params=pltpu.CompilerParams(vmem_limit_bytes=32 * 2**20),
        name="unpack",
    )(back)


def solution(mesh):
    rows = P(("dp", "blk"), None)
    return jax.shard_map(
        local,
        mesh=mesh,
        in_specs=(rows, rows, rows, rows, rows, P(("dp", "blk"))),
        out_specs=(rows, rows, rows),
        check_vma=False,
    )
```

time: 116 us -> 107 us (0.922)
  local copies, waits for them, and re-layouts: 6.3 us -> 0 us
  Pallas kernels: 23.8 us -> 22 us
    unnamed x10 -> x0, local copies, waits for them, and re-layouts: 6.21 us -> none
    pallas_call x1, Pallas kernels: 18.2 us -> 13.9 us  [local(): pl.pallas_call(attention_kernel, out_shape=jax.ShapeDtypeStruct((BLOCKS,...]
    pallas_call x2, Pallas kernels: 5.56 us -> 8.13 us  [the longest x1 6.34 us: local(): pl.pallas_call(pack_kernel, in_specs=[hbm] * 5 + [vmem], out_specs=hbm, o...]
where the time goes in v2:
time: 107 us
  blocking collectives  84 us (79%)
  Pallas kernels  22 us (21%)
    all_to_all x1, blocking collectives, local(): payload = lax.all_to_all(packed, 'blk', 0, 0, tiled=True)  53.4 us
    all_to_all x1, blocking collectives, local(): back = lax.all_to_all(result, 'blk', 0, 0, tiled=True)  30.6 us
    pallas_call x1, Pallas kernels, local(): pl.pallas_call(attention_kernel, out_shape=jax.ShapeDtypeStruct((BLOCKS,...  13.9 us
    pallas_call x1, Pallas kernels, local(): pl.pallas_call(pack_kernel, in_specs=[hbm] * 5 + [vmem], out_specs=hbm, o...  6.34 us

profile of v2, /device:TPU:0, one launch (start us, length us, event | category | flops | bytes accessed | tf_op | source)
XLA Modules:
  0.0 106.7 jit_solution(14863626932982870911)
XLA Ops:
  0.6 6.3 %pack.1 = bf16[8,1936,128]{2,1,0:T(8,128)(2,1)} custom-call(bf16[192,4096]{1,0:T(8,128)(2,1)} %q_ref.1, bf16[192,1024]{1,0:T(8,128)(2,1)} %k_ref.1, bf16[192,1024]{1,0:T(8,128)(2,1)} %v_ref.1, bf16[192,4096]{1,0:T(8,128)(2,1)} %o_ref.1, bf16[192,4096]{1,0:T(8,128)(2,1)} %g_ref.1, s32[1,192]{1,0:T(1,128)} %bitcast.1), custom_call_target="tpu_custom_call" | custom-call | tf_op jit(solution)/shard_map/pack/pallas_call | solution.py:168
  7.0 53.4 %all_to_all.10.pay_ref = bf16[8,1936,128]{2,1,0:T(8,128)(2,1)S(1)} all-to-all(bf16[8,1936,128]{2,1,0:T(8,128)(2,1)} %pack.1), channel_id=1, replica_groups=mesh['dp'=16,'blk'=8] {'blk'}, dimensions={0} | all-to-all | bytes 7929856 | tf_op jit(solution)/shard_map/all_to_all | solution.py:183
  60.4 13.9 %attention.1 = bf16[8,1152,128]{2,1,0:T(8,128)(2,1)S(1)} custom-call(bf16[8,1936,128]{2,1,0:T(8,128)(2,1)S(1)} %all_to_all.10.pay_ref), custom_call_target="tpu_custom_call" | custom-call | tf_op jit(solution)/shard_map/attention/pallas_call | solution.py:184
  74.3 30.6 %all_to_all.11.back_ref = bf16[8,1152,128]{2,1,0:T(8,128)(2,1)S(1)} all-to-all(bf16[8,1152,128]{2,1,0:T(8,128)(2,1)S(1)} %attention.1), channel_id=1, replica_groups=mesh['dp'=16,'blk'=8] {'blk'}, dimensions={0} | all-to-all | bytes 4718592 | tf_op jit(solution)/shard_map/all_to_all | solution.py:197
  104.9 1.8 %unpack.1 = (bf16[192,4096]{1,0:T(8,128)(2,1)}, bf16[192,1024]{1,0:T(8,128)(2,1)}, bf16[192,1024]{1,0:T(8,128)(2,1)}) custom-call(bf16[8,1152,128]{2,1,0:T(8,128)(2,1)S(1)} %all_to_all.11.back_ref), custom_call_target="tpu_custom_call" | custom-call | tf_op jit(solution)/shard_map/unpack/pallas_call | solution.py:198

commit v3 on v2

v3 whole, which is shorter than its diff:
```python
import functools
import math

import jax
import jax.numpy as jnp
from jax import lax
from jax.experimental import pallas as pl
from jax.experimental.pallas import tpu as pltpu
from jax.sharding import PartitionSpec as P

QUERY_HEADS = 32
KEY_VALUE_HEADS = 8
HEAD_WIDTH = 128
GROUP = QUERY_HEADS // KEY_VALUE_HEADS
DOCS = 8
TOK = 192
BLOCKS = 8
MOST_BLOCKS = 5
UNIT = 64
UNITS = TOK // UNIT
LANES = GROUP * UNIT
Q_AT = 0
G_AT = GROUP * TOK
K_AT = 2 * GROUP * TOK
V_AT = K_AT + TOK
X_AT = V_AT + TOK
SEND_ROWS = X_AT + 16
BACK_ROWS = (GROUP + 2) * TOK
NT = (((1,), (1,)), ((), ()))
TN = (((0,), (0,)), ((), ()))
NN = (((1,), (0,)), ((), ()))


def dot(a, b, dims):
    return lax.dot_general(a, b, dims, preferred_element_type=jnp.float32)


def pack_kernel(
    q_ref, k_ref, v_ref, o_ref, g_ref, doc_ref, out_ref, q_buf, k_buf, v_buf, o_buf, g_buf, doc_buf, send, in_sem, kv_sem, sem
):
    whole = [
        pltpu.make_async_copy(k_ref, k_buf, kv_sem.at[0]),
        pltpu.make_async_copy(v_ref, v_buf, kv_sem.at[1]),
        pltpu.make_async_copy(doc_ref, doc_buf, kv_sem.at[2]),
    ]
    arrivals = []
    for group in range(KEY_VALUE_HEADS):
        cols = slice(group * GROUP * HEAD_WIDTH, (group + 1) * GROUP * HEAD_WIDTH)
        arrivals.append(
            [
                pltpu.make_async_copy(ref.at[:, cols], buf.at[:, cols], in_sem.at[n, group])
                for n, (ref, buf) in enumerate(((g_ref, g_buf), (o_ref, o_buf), (q_ref, q_buf)))
            ]
        )
        for copy in arrivals[group]:
            copy.start()
        if group == 0:
            for copy in whole:
                copy.start()
    departures = []
    for group in range(KEY_VALUE_HEADS):
        for copy in arrivals[group]:
            copy.wait()
        if group == 0:
            for copy in whole:
                copy.wait()
            doc = doc_buf[...].astype(jnp.float32)
            tail = [doc[:, t * UNIT : (t + 1) * UNIT] for t in range(UNITS)]
            tail = [jnp.concatenate([part, part], axis=1) for part in tail]
            tail = jnp.concatenate(tail + [jnp.zeros((1, 128), jnp.float32)], axis=0)
        product = []
        for t in range(UNITS):
            rows = slice(t * UNIT, (t + 1) * UNIT)
            for h in range(GROUP):
                head = group * GROUP + h
                cols = slice(head * HEAD_WIDTH, (head + 1) * HEAD_WIDTH)
                at = t * LANES + h * UNIT
                g = g_buf[rows, cols]
                send[group, Q_AT + at : Q_AT + at + UNIT, :] = q_buf[rows, cols]
                send[group, G_AT + at : G_AT + at + UNIT, :] = g
                product.append(g.astype(jnp.float32) * o_buf[rows, cols].astype(jnp.float32))
        own = slice(group * HEAD_WIDTH, (group + 1) * HEAD_WIDTH)
        send[group, K_AT : K_AT + TOK, :] = k_buf[:, own]
        send[group, V_AT : V_AT + TOK, :] = v_buf[:, own]
        delta = jnp.sum(jnp.concatenate(product, axis=0).T, axis=0, keepdims=True)
        delta = jnp.concatenate([delta[:, t * 128 : (t + 1) * 128] for t in range(6)], axis=0)
        high = delta.astype(jnp.bfloat16).astype(jnp.float32)
        extra = jnp.concatenate([high, delta - high, tail], axis=0)
        send[group, X_AT : X_AT + 16, :] = extra.astype(jnp.bfloat16)
        departures.append(pltpu.make_async_copy(send.at[group], out_ref.at[group], sem.at[group]))
        departures[group].start()
    for copy in departures:
        copy.wait()


def attention_kernel(pay_ref, out_ref, extra_ref, start_ref, first_ref, dk_ref, dv_ref):
    scale = 1.0 / math.sqrt(HEAD_WIDTH)
    to_exp2 = scale * math.log2(math.e)
    dk_ref[...] = jnp.zeros_like(dk_ref)
    dv_ref[...] = jnp.zeros_like(dv_ref)
    for b in range(BLOCKS):
        extra_ref[b] = pay_ref[b, X_AT : X_AT + 16, :].astype(jnp.float32)
    docs = jnp.concatenate([extra_ref[b, 12:15, :] for b in range(BLOCKS)], axis=0)
    starts = jnp.zeros_like(docs)
    for d in range(1, DOCS):
        before = 0.5 * jnp.sum(jnp.where(docs < d, 1.0, 0.0), keepdims=True)
        starts = jnp.where(docs == d, before, starts)
    for b in range(BLOCKS):
        own = starts[UNITS * b : UNITS * (b + 1)]
        start_ref[b] = jnp.concatenate([own, own, own[:2]], axis=0)
        first_ref[b] = jnp.min(own).astype(jnp.int32)

    def query_block(i, carry):
        first_block = first_ref[i] // TOK
        start3 = start_ref[i].astype(jnp.int32)
        delta6 = extra_ref[i, 0:6, :] + extra_ref[i, 6:12, :]

        def with_blocks(count):
            low = i - count + 1
            row0 = pl.multiple_of(low * TOK, TOK)
            keys = pay_ref[pl.ds(low, count), K_AT : K_AT + TOK, :].reshape(count * TOK, HEAD_WIDTH)
            values = pay_ref[pl.ds(low, count), V_AT : V_AT + TOK, :].reshape(
                count * TOK, HEAD_WIDTH
            )
            token = lax.broadcasted_iota(jnp.int32, (UNIT, LANES), 1) % UNIT
            causal = lax.broadcasted_iota(jnp.int32, (UNIT, LANES), 0) <= token

            def load(t, at):
                return pay_ref[i, at + t * LANES : at + (t + 1) * LANES, :]

            def rows_at(t, j):
                return TOK if j + 1 < count else (t + 1) * UNIT

            def scores_of(t, j):
                return dot(keys[j * TOK : j * TOK + rows_at(t, j)], load(t, Q_AT), NT)

            def weigh(t, j, scores):
                rows = rows_at(t, j)
                start = jnp.concatenate([start3[t : t + 1]] * 2, axis=1) - (low + j) * TOK
                key_row = lax.broadcasted_iota(jnp.int32, (rows, LANES), 0)
                scores = jnp.where(key_row >= start, scores, -1e30)
                if j + 1 == count:
                    edge = jnp.where(causal, scores[rows - UNIT :], -1e30)
                    scores = jnp.concatenate([scores[: rows - UNIT], edge], axis=0) if t else edge
                top = jnp.max(scores, axis=0, keepdims=True) * to_exp2
                weights = jnp.exp2(scores * to_exp2 - top)
                return weights, top, jnp.sum(weights, axis=0, keepdims=True)

            def factors(parts):
                top = functools.reduce(jnp.maximum, [part[1] for part in parts])
                shares = [jnp.exp2(part[1] - top) for part in parts]
                total = functools.reduce(
                    jnp.add, [share * part[2] for share, part in zip(shares, parts)]
                )
                inverse = 1.0 / total
                return [share * inverse for share in shares]

            def grads(t, j, weights, factor, prob_grad):
                delta = jnp.concatenate(
                    [delta6[2 * t : 2 * t + 1], delta6[2 * t + 1 : 2 * t + 2]], axis=1
                )
                probs = weights * factor
                return probs.astype(jnp.bfloat16), (probs * (prob_grad - delta)).astype(jnp.bfloat16)

            def prob_grad_of(t, j):
                return dot(values[j * TOK : j * TOK + rows_at(t, j)], load(t, G_AT), NT)

            def accumulate(t, j, probs, score_grad):
                rows = rows_at(t, j)
                at = pl.ds(pl.multiple_of(row0 + j * TOK, UNIT), rows)
                dv_ref[at] += dot(probs, load(t, G_AT), NN)
                dk_ref[at] += dot(score_grad, load(t, Q_AT), NN)

            def finish(t, score_grads):
                rows = (count - 1) * TOK + (t + 1) * UNIT
                score_grad = jnp.concatenate(score_grads, axis=0) if count > 1 else score_grads[0]
                dq = (dot(keys[:rows], score_grad, TN) * scale).T.astype(jnp.bfloat16)
                for h in range(GROUP):
                    at = h * TOK + t * UNIT
                    out_ref[i, at : at + UNIT, :] = dq[h * UNIT : (h + 1) * UNIT]

            blocks = range(count)
            parts = []
            for t in range(UNITS):
                ahead = scores_of(t, 0)
                parts.append([])
                for j in blocks:
                    now, ahead = ahead, scores_of(t, j + 1) if j + 1 < count else None
                    parts[t].append(weigh(t, j, now))
            factor = [factors(part) for part in parts]
            steps = [(t, j) for t in range(UNITS) for j in blocks]
            ahead = prob_grad_of(*steps[0])
            done = {}
            for n, step in enumerate(steps):
                t, j = step
                now, ahead = ahead, prob_grad_of(*steps[n + 1]) if n + 1 < len(steps) else None
                done[step] = grads(t, j, parts[t][j][0], factor[t][j], now)
                if n:
                    accumulate(*steps[n - 1], *done[steps[n - 1]])
                if j + 1 == count:
                    finish(t, [done[t, k][1] for k in blocks])
            accumulate(*steps[-1], *done[steps[-1]])

        for count in range(1, MOST_BLOCKS + 1):
            pl.when(i - first_block + 1 == count)(lambda count=count: with_blocks(count))
        return carry

    lax.fori_loop(0, BLOCKS, query_block, 0)
    at = GROUP * TOK
    for b in range(BLOCKS):
        own = slice(b * TOK, (b + 1) * TOK)
        out_ref[b, at : at + TOK, :] = (dk_ref[own] * scale).astype(jnp.bfloat16)
        out_ref[b, at + TOK : at + 2 * TOK, :] = dv_ref[own].astype(jnp.bfloat16)


def unpack_kernel(back_ref, dq_ref, dk_ref, dv_ref, sem):
    copies = []

    def send(group, at, ref, column):
        copies.append(
            pltpu.make_async_copy(
                back_ref.at[group, pl.ds(at, TOK)],
                ref.at[:, column * HEAD_WIDTH : (column + 1) * HEAD_WIDTH],
                sem.at[len(copies)],
            )
        )

    for group in range(KEY_VALUE_HEADS):
        for h in range(GROUP):
            send(group, h * TOK, dq_ref, group * GROUP + h)
        send(group, GROUP * TOK, dk_ref, group)
        send(group, (GROUP + 1) * TOK, dv_ref, group)
    for copy in copies:
        copy.start()
    for copy in copies:
        copy.wait()


def local(queries, keys, values, outputs, output_gradient, doc_ids):
    hbm = pl.BlockSpec(memory_space=pltpu.HBM)
    packed = pl.pallas_call(
        pack_kernel,
        in_specs=[hbm] * 6,
        out_specs=hbm,
        out_shape=jax.ShapeDtypeStruct((KEY_VALUE_HEADS, SEND_ROWS, 128), jnp.bfloat16),
        scratch_shapes=[
            pltpu.VMEM(queries.shape, jnp.bfloat16),
            pltpu.VMEM(keys.shape, jnp.bfloat16),
            pltpu.VMEM(values.shape, jnp.bfloat16),
            pltpu.VMEM(outputs.shape, jnp.bfloat16),
            pltpu.VMEM(output_gradient.shape, jnp.bfloat16),
            pltpu.VMEM((1, TOK), jnp.int32),
            pltpu.VMEM((KEY_VALUE_HEADS, SEND_ROWS, 128), jnp.bfloat16),
            pltpu.SemaphoreType.DMA((3, KEY_VALUE_HEADS)),
            pltpu.SemaphoreType.DMA((3,)),
            pltpu.SemaphoreType.DMA((KEY_VALUE_HEADS,)),
        ],
        compiler_params=pltpu.CompilerParams(vmem_limit_bytes=62 * 2**20),
        name="pack",
    )(queries, keys, values, outputs, output_gradient, doc_ids.reshape(1, TOK))
    payload = lax.all_to_all(packed, "blk", 0, 0, tiled=True)
    result = pl.pallas_call(
        attention_kernel,
        out_shape=jax.ShapeDtypeStruct((BLOCKS, BACK_ROWS, 128), jnp.bfloat16),
        scratch_shapes=[
            pltpu.VMEM((BLOCKS, 16, 128), jnp.float32),
            pltpu.VMEM((BLOCKS, 8, 128), jnp.float32),
            pltpu.SMEM((BLOCKS,), jnp.int32),
            pltpu.VMEM((BLOCKS * TOK, HEAD_WIDTH), jnp.float32),
            pltpu.VMEM((BLOCKS * TOK, HEAD_WIDTH), jnp.float32),
        ],
        compiler_params=pltpu.CompilerParams(vmem_limit_bytes=32 * 2**20),
        name="attention",
    )(payload)
    back = lax.all_to_all(result, "blk", 0, 0, tiled=True)
    return pl.pallas_call(
        unpack_kernel,
        in_specs=[pl.BlockSpec(memory_space=pl.ANY)],
        out_specs=[hbm] * 3,
        out_shape=[
            jax.ShapeDtypeStruct(queries.shape, jnp.bfloat16),
            jax.ShapeDtypeStruct(keys.shape, jnp.bfloat16),
            jax.ShapeDtypeStruct(values.shape, jnp.bfloat16),
        ],
        scratch_shapes=[pltpu.SemaphoreType.DMA((QUERY_HEADS + 2 * KEY_VALUE_HEADS,))],
        compiler_params=pltpu.CompilerParams(vmem_limit_bytes=32 * 2**20),
        name="unpack",
    )(back)


def solution(mesh):
    rows = P(("dp", "blk"), None)
    return jax.shard_map(
        local,
        mesh=mesh,
        in_specs=(rows, rows, rows, rows, rows, P(("dp", "blk"))),
        out_specs=(rows, rows, rows),
        check_vma=False,
    )
```

time: 107 us -> 104 us (0.972)
  Pallas kernels: 22 us -> 18.9 us
    pallas_call x1, Pallas kernels: 13.9 us -> 11.8 us  [local(): pl.pallas_call(attention_kernel, out_shape=jax.ShapeDtypeStruct((BLOCKS,...]
    pallas_call x1, Pallas kernels: 6.34 us -> 5.23 us  [local(): pl.pallas_call(pack_kernel, in_specs=[hbm] * 6, out_specs=hbm, out_shape=...]
where the time goes in v3:
time: 104 us; the launch traced here: 103 us
  blocking collectives  84 us (81%)
  Pallas kernels  18.9 us (18%)
    all_to_all x1, blocking collectives, local(): payload = lax.all_to_all(packed, 'blk', 0, 0, tiled=True)  53.4 us
    all_to_all x1, blocking collectives, local(): back = lax.all_to_all(result, 'blk', 0, 0, tiled=True)  30.6 us
    pallas_call x1, Pallas kernels, local(): pl.pallas_call(attention_kernel, out_shape=jax.ShapeDtypeStruct((BLOCKS,...  11.8 us
    pallas_call x1, Pallas kernels, local(): pl.pallas_call(pack_kernel, in_specs=[hbm] * 6, out_specs=hbm, out_shape=...  5.23 us

profile of v3, /device:TPU:0, one launch (start us, length us, event | category | flops | bytes accessed | tf_op | source)
XLA Modules:
  0.0 103.5 jit_solution(3077625198080190743)
XLA Ops:
  0.6 5.2 %pack.1 = bf16[8,1936,128]{2,1,0:T(8,128)(2,1)} custom-call(bf16[192,4096]{1,0:T(8,128)(2,1)} %q_ref.1, bf16[192,1024]{1,0:T(8,128)(2,1)} %k_ref.1, bf16[192,1024]{1,0:T(8,128)(2,1)} %v_ref.1, bf16[192,4096]{1,0:T(8,128)(2,1)} %o_ref.1, bf16[192,4096]{1,0:T(8,128)(2,1)} %g_ref.1, s32[1,192]{1,0:T(1,128)} %bitcast.1), custom_call_target="tpu_custom_call" | custom-call | tf_op jit(solution)/shard_map/pack/pallas_call | solution.py:241
  5.9 53.4 %all_to_all.10.pay_ref = bf16[8,1936,128]{2,1,0:T(8,128)(2,1)S(1)} all-to-all(bf16[8,1936,128]{2,1,0:T(8,128)(2,1)} %pack.1), channel_id=1, replica_groups=mesh['dp'=16,'blk'=8] {'blk'}, dimensions={0} | all-to-all | bytes 7929856 | tf_op jit(solution)/shard_map/all_to_all | solution.py:261
  59.3 11.8 %attention.1 = bf16[8,1152,128]{2,1,0:T(8,128)(2,1)S(1)} custom-call(bf16[8,1936,128]{2,1,0:T(8,128)(2,1)S(1)} %all_to_all.10.pay_ref), custom_call_target="tpu_custom_call" | custom-call | tf_op jit(solution)/shard_map/attention/pallas_call | solution.py:262
  71.1 30.6 %all_to_all.11.back_ref = bf16[8,1152,128]{2,1,0:T(8,128)(2,1)S(1)} all-to-all(bf16[8,1152,128]{2,1,0:T(8,128)(2,1)S(1)} %attention.1), channel_id=1, replica_groups=mesh['dp'=16,'blk'=8] {'blk'}, dimensions={0} | all-to-all | bytes 4718592 | tf_op jit(solution)/shard_map/all_to_all | solution.py:275
  101.7 1.8 %unpack.1 = (bf16[192,4096]{1,0:T(8,128)(2,1)}, bf16[192,1024]{1,0:T(8,128)(2,1)}, bf16[192,1024]{1,0:T(8,128)(2,1)}) custom-call(bf16[8,1152,128]{2,1,0:T(8,128)(2,1)S(1)} %all_to_all.11.back_ref), custom_call_target="tpu_custom_call" | custom-call | tf_op jit(solution)/shard_map/unpack/pallas_call | solution.py:276

commit v4 on v3

--- a/solution.py
+++ b/solution.py
@@ -19,6 +19,9 @@
 UNIT = 64
 UNITS = TOK // UNIT
 LANES = GROUP * UNIT
+KINDS = MOST_BLOCKS + 1
+TOGETHER = [(n, n + 1) for n in range(1, MOST_BLOCKS)] + [(n, 0) for n in range(KINDS)]
+SHORT = 3 * UNIT
 Q_AT = 0
 G_AT = GROUP * TOK
 K_AT = 2 * GROUP * TOK
@@ -93,7 +96,9 @@
         copy.wait()
 
 
-def attention_kernel(pay_ref, out_ref, extra_ref, start_ref, first_ref, dk_ref, dv_ref):
+def attention_kernel(
+    pay_ref, out_ref, extra_ref, start_ref, first_ref, reach_ref, dk_ref, dv_ref
+):
     scale = 1.0 / math.sqrt(HEAD_WIDTH)
     to_exp2 = scale * math.log2(math.e)
     dk_ref[...] = jnp.zeros_like(dk_ref)
@@ -109,103 +114,151 @@
         own = starts[UNITS * b : UNITS * (b + 1)]
         start_ref[b] = jnp.concatenate([own, own, own[:2]], axis=0)
         first_ref[b] = jnp.min(own).astype(jnp.int32)
-
-    def query_block(i, carry):
+        chunk_at = b * TOK + UNIT * lax.broadcasted_iota(jnp.int32, own.shape, 0)
+        reach_ref[b] = jnp.max(chunk_at.astype(jnp.float32) - own).astype(jnp.int32)
+
+    def kind_of(i):
         first_block = first_ref[i] // TOK
+        is_short = (i > 0) & (reach_ref[i] <= SHORT - UNIT) & (first_block < i)
+        return jnp.where(is_short, 0, i - first_block + 1)
+
+    def chunks_of(i, kind):
+        short = kind == 0
+        count = kind or 2
         start3 = start_ref[i].astype(jnp.int32)
         delta6 = extra_ref[i, 0:6, :] + extra_ref[i, 6:12, :]
-
-        def with_blocks(count):
-            low = i - count + 1
-            row0 = pl.multiple_of(low * TOK, TOK)
-            keys = pay_ref[pl.ds(low, count), K_AT : K_AT + TOK, :].reshape(count * TOK, HEAD_WIDTH)
-            values = pay_ref[pl.ds(low, count), V_AT : V_AT + TOK, :].reshape(
-                count * TOK, HEAD_WIDTH
-            )
-            token = lax.broadcasted_iota(jnp.int32, (UNIT, LANES), 1) % UNIT
-            causal = lax.broadcasted_iota(jnp.int32, (UNIT, LANES), 0) <= token
-
-            def load(t, at):
-                return pay_ref[i, at + t * LANES : at + (t + 1) * LANES, :]
-
-            def rows_at(t, j):
-                return TOK if j + 1 < count else (t + 1) * UNIT
-
-            def scores_of(t, j):
-                return dot(keys[j * TOK : j * TOK + rows_at(t, j)], load(t, Q_AT), NT)
-
-            def weigh(t, j, scores):
-                rows = rows_at(t, j)
-                start = jnp.concatenate([start3[t : t + 1]] * 2, axis=1) - (low + j) * TOK
+        low = i - count + 1
+        row0 = pl.multiple_of(low * TOK, TOK)
+        keys = pay_ref[pl.ds(low, count), K_AT : K_AT + TOK, :].reshape(count * TOK, HEAD_WIDTH)
+        values = pay_ref[pl.ds(low, count), V_AT : V_AT + TOK, :].reshape(
+            count * TOK, HEAD_WIDTH
+        )
+        token = lax.broadcasted_iota(jnp.int32, (UNIT, LANES), 1) % UNIT
+        causal = lax.broadcasted_iota(jnp.int32, (UNIT, LANES), 0) <= token
+
+        def load(t, at):
+            return pay_ref[i, at + t * LANES : at + (t + 1) * LANES, :]
+
+        def end(t):
+            return (count - 1) * TOK + (t + 1) * UNIT
+
+        def begin(t):
+            return end(t) - SHORT if short else 0
+
+        def pieces(t):
+            edges = list(range(begin(t), end(t), TOK)) + [end(t)]
+            return [slice(p - begin(t), q - begin(t)) for p, q in zip(edges, edges[1:])]
+
+        def scores_of(t):
+            return dot(keys[begin(t) : end(t)], load(t, Q_AT), NT)
+
+        def prob_grad_of(t):
+            return dot(values[begin(t) : end(t)], load(t, G_AT), NT)
+
+        def weigh(t, scores):
+            start = jnp.concatenate([start3[t : t + 1]] * 2, axis=1) - (low * TOK + begin(t))
+            parts = []
+            for piece in pieces(t):
+                rows = piece.stop - piece.start
                 key_row = lax.broadcasted_iota(jnp.int32, (rows, LANES), 0)
-                scores = jnp.where(key_row >= start, scores, -1e30)
-                if j + 1 == count:
-                    edge = jnp.where(causal, scores[rows - UNIT :], -1e30)
-                    scores = jnp.concatenate([scores[: rows - UNIT], edge], axis=0) if t else edge
-                top = jnp.max(scores, axis=0, keepdims=True) * to_exp2
-                weights = jnp.exp2(scores * to_exp2 - top)
-                return weights, top, jnp.sum(weights, axis=0, keepdims=True)
-
-            def factors(parts):
-                top = functools.reduce(jnp.maximum, [part[1] for part in parts])
-                shares = [jnp.exp2(part[1] - top) for part in parts]
-                total = functools.reduce(
-                    jnp.add, [share * part[2] for share, part in zip(shares, parts)]
-                )
-                inverse = 1.0 / total
-                return [share * inverse for share in shares]
-
-            def grads(t, j, weights, factor, prob_grad):
-                delta = jnp.concatenate(
-                    [delta6[2 * t : 2 * t + 1], delta6[2 * t + 1 : 2 * t + 2]], axis=1
-                )
-                probs = weights * factor
-                return probs.astype(jnp.bfloat16), (probs * (prob_grad - delta)).astype(jnp.bfloat16)
-
-            def prob_grad_of(t, j):
-                return dot(values[j * TOK : j * TOK + rows_at(t, j)], load(t, G_AT), NT)
-
-            def accumulate(t, j, probs, score_grad):
-                rows = rows_at(t, j)
-                at = pl.ds(pl.multiple_of(row0 + j * TOK, UNIT), rows)
-                dv_ref[at] += dot(probs, load(t, G_AT), NN)
-                dk_ref[at] += dot(score_grad, load(t, Q_AT), NN)
-
-            def finish(t, score_grads):
-                rows = (count - 1) * TOK + (t + 1) * UNIT
-                score_grad = jnp.concatenate(score_grads, axis=0) if count > 1 else score_grads[0]
-                dq = (dot(keys[:rows], score_grad, TN) * scale).T.astype(jnp.bfloat16)
-                for h in range(GROUP):
-                    at = h * TOK + t * UNIT
-                    out_ref[i, at : at + UNIT, :] = dq[h * UNIT : (h + 1) * UNIT]
-
-            blocks = range(count)
-            parts = []
-            for t in range(UNITS):
-                ahead = scores_of(t, 0)
-                parts.append([])
-                for j in blocks:
-                    now, ahead = ahead, scores_of(t, j + 1) if j + 1 < count else None
-                    parts[t].append(weigh(t, j, now))
-            factor = [factors(part) for part in parts]
-            steps = [(t, j) for t in range(UNITS) for j in blocks]
-            ahead = prob_grad_of(*steps[0])
-            done = {}
-            for n, step in enumerate(steps):
-                t, j = step
-                now, ahead = ahead, prob_grad_of(*steps[n + 1]) if n + 1 < len(steps) else None
-                done[step] = grads(t, j, parts[t][j][0], factor[t][j], now)
-                if n:
-                    accumulate(*steps[n - 1], *done[steps[n - 1]])
-                if j + 1 == count:
-                    finish(t, [done[t, k][1] for k in blocks])
-            accumulate(*steps[-1], *done[steps[-1]])
-
-        for count in range(1, MOST_BLOCKS + 1):
-            pl.when(i - first_block + 1 == count)(lambda count=count: with_blocks(count))
+                part = jnp.where(key_row >= start - piece.start, scores[piece], -1e30)
+                if piece.stop == end(t) - begin(t):
+                    edge = jnp.where(causal, part[rows - UNIT :], -1e30)
+                    part = jnp.concatenate([part[: rows - UNIT], edge], axis=0) if rows > UNIT else edge
+                top = jnp.max(part, axis=0, keepdims=True) * to_exp2
+                weights = jnp.exp2(part * to_exp2 - top)
+                parts.append((weights, top, jnp.sum(weights, axis=0, keepdims=True)))
+            return parts
+
+        def factors(parts):
+            top = functools.reduce(jnp.maximum, [part[1] for part in parts])
+            shares = [jnp.exp2(part[1] - top) for part in parts]
+            total = functools.reduce(
+                jnp.add, [share * part[2] for share, part in zip(shares, parts)]
+            )
+            inverse = 1.0 / total
+            return [share * inverse for share in shares]
+
+        def grads(t, parts, prob_grad):
+            delta = jnp.concatenate(
+                [delta6[2 * t : 2 * t + 1], delta6[2 * t + 1 : 2 * t + 2]], axis=1
+            )
+            low_probs, score_grads = [], []
+            for piece, part, factor in zip(pieces(t), parts, factors(parts)):
+                probs = part[0] * factor
+                low_probs.append(probs.astype(jnp.bfloat16))
+                score_grads.append((probs * (prob_grad[piece] - delta)).astype(jnp.bfloat16))
+            if len(parts) == 1:
+                return low_probs[0], score_grads[0]
+            return jnp.concatenate(low_probs, axis=0), jnp.concatenate(score_grads, axis=0)
+
+        def finish(t, probs, score_grad):
+            at = pl.ds(pl.multiple_of(row0 + begin(t), UNIT), end(t) - begin(t))
+            dv_ref[at] += dot(probs, load(t, G_AT), NN)
+            dk_ref[at] += dot(score_grad, load(t, Q_AT), NN)
+            dq = dot(keys[begin(t) : end(t)], score_grad, TN) * scale
+            dq = dq.T.astype(jnp.bfloat16)
+            for h in range(GROUP):
+                at = h * TOK + t * UNIT
+                out_ref[i, at : at + UNIT, :] = dq[h * UNIT : (h + 1) * UNIT]
+
+        def chunk(t):
+            return tuple(
+                functools.partial(step, t)
+                for step in (scores_of, prob_grad_of, weigh, grads, finish)
+            )
+
+        return [chunk(t) for t in range(UNITS)]
+
+    def run(chunks):
+        count = len(chunks)
+        s, d, w, g = {}, {}, {}, {}
+
+        def scores_of(n):
+            s[n] = chunks[n][0]()
+
+        def grads(n):
+            g[n] = chunks[n][3](w.pop(n), d.pop(n))
+
+        scores_of(0)
+        scores_of(1)
+        for n in range(count):
+            w[n] = chunks[n][2](s.pop(n))
+            if n + 2 < count:
+                scores_of(n + 2)
+            d[n] = chunks[n][1]()
+            if n > 1:
+                chunks[n - 2][4](*g.pop(n - 2))
+            if n > 0:
+                grads(n - 1)
+        chunks[-2][4](*g.pop(count - 2))
+        grads(count - 1)
+        chunks[-1][4](*g.pop(count - 1))
+
+    def two_blocks(p, carry):
+        first, second = kind_of(2 * p), kind_of(2 * p + 1)
+        code = first * KINDS + second
+        alone = code >= 0
+        for one, two in TOGETHER:
+            match = code == one * KINDS + two
+            alone = alone & jnp.logical_not(match)
+            pl.when(match)(
+                lambda one=one, two=two: run(chunks_of(2 * p, one) + chunks_of(2 * p + 1, two))
+            )
+
+        @pl.when(alone)
+        def _():
+            def one_block(i, carry):
+                kind = kind_of(i)
+                for value in range(KINDS):
+                    pl.when(kind == value)(lambda value=value: run(chunks_of(i, value)))
+                return carry
+
+            lax.fori_loop(2 * p, 2 * p + 2, one_block, 0)
+
         return carry
 
-    lax.fori_loop(0, BLOCKS, query_block, 0)
+    lax.fori_loop(0, BLOCKS // 2, two_blocks, 0)
     at = GROUP * TOK
     for b in range(BLOCKS):
         own = slice(b * TOK, (b + 1) * TOK)
@@ -266,6 +319,7 @@
             pltpu.VMEM((BLOCKS, 16, 128), jnp.float32),
             pltpu.VMEM((BLOCKS, 8, 128), jnp.float32),
             pltpu.SMEM((BLOCKS,), jnp.int32),
+            pltpu.SMEM((BLOCKS,), jnp.int32),
             pltpu.VMEM((BLOCKS * TOK, HEAD_WIDTH), jnp.float32),
             pltpu.VMEM((BLOCKS * TOK, HEAD_WIDTH), jnp.float32),
         ],

time: 104 us -> 101 us (0.971)
  Pallas kernels: 18.9 us -> 16.4 us
    pallas_call x1, Pallas kernels: 11.8 us -> 9.35 us  [local(): pl.pallas_call(attention_kernel, out_shape=jax.ShapeDtypeStruct((BLOCKS,...]
where the time goes in v4:
time: 101 us
  blocking collectives  84 us (83%)
  Pallas kernels  16.4 us (16%)
    all_to_all x1, blocking collectives, local(): payload = lax.all_to_all(packed, 'blk', 0, 0, tiled=True)  53.4 us
    all_to_all x1, blocking collectives, local(): back = lax.all_to_all(result, 'blk', 0, 0, tiled=True)  30.6 us
    pallas_call x1, Pallas kernels, local(): pl.pallas_call(attention_kernel, out_shape=jax.ShapeDtypeStruct((BLOCKS,...  9.35 us
    pallas_call x1, Pallas kernels, local(): pl.pallas_call(pack_kernel, in_specs=[hbm] * 6, out_specs=hbm, out_shape=...  5.23 us

profile of v4, /device:TPU:0, one launch (start us, length us, event | category | flops | bytes accessed | tf_op | source)
XLA Modules:
  0.0 101.0 jit_solution(881569923100094002)
XLA Ops:
  0.6 5.2 %pack.1 = bf16[8,1936,128]{2,1,0:T(8,128)(2,1)} custom-call(bf16[192,4096]{1,0:T(8,128)(2,1)} %q_ref.1, bf16[192,1024]{1,0:T(8,128)(2,1)} %k_ref.1, bf16[192,1024]{1,0:T(8,128)(2,1)} %v_ref.1, bf16[192,4096]{1,0:T(8,128)(2,1)} %o_ref.1, bf16[192,4096]{1,0:T(8,128)(2,1)} %g_ref.1, s32[1,192]{1,0:T(1,128)} %bitcast.1), custom_call_target="tpu_custom_call" | custom-call | tf_op jit(solution)/shard_map/pack/pallas_call | solution.py:294
  5.9 53.4 %all_to_all.10.pay_ref = bf16[8,1936,128]{2,1,0:T(8,128)(2,1)S(1)} all-to-all(bf16[8,1936,128]{2,1,0:T(8,128)(2,1)} %pack.1), channel_id=1, replica_groups=mesh['dp'=16,'blk'=8] {'blk'}, dimensions={0} | all-to-all | bytes 7929856 | tf_op jit(solution)/shard_map/all_to_all | solution.py:314
  59.3 9.3 %attention.1 = bf16[8,1152,128]{2,1,0:T(8,128)(2,1)S(1)} custom-call(bf16[8,1936,128]{2,1,0:T(8,128)(2,1)S(1)} %all_to_all.10.pay_ref), custom_call_target="tpu_custom_call" | custom-call | tf_op jit(solution)/shard_map/attention/pallas_call | solution.py:315
  68.7 30.6 %all_to_all.11.back_ref = bf16[8,1152,128]{2,1,0:T(8,128)(2,1)S(1)} all-to-all(bf16[8,1152,128]{2,1,0:T(8,128)(2,1)S(1)} %attention.1), channel_id=1, replica_groups=mesh['dp'=16,'blk'=8] {'blk'}, dimensions={0} | all-to-all | bytes 4718592 | tf_op jit(solution)/shard_map/all_to_all | solution.py:329
  99.2 1.8 %unpack.1 = (bf16[192,4096]{1,0:T(8,128)(2,1)}, bf16[192,1024]{1,0:T(8,128)(2,1)}, bf16[192,1024]{1,0:T(8,128)(2,1)}) custom-call(bf16[8,1152,128]{2,1,0:T(8,128)(2,1)S(1)} %all_to_all.11.back_ref), custom_call_target="tpu_custom_call" | custom-call | tf_op jit(solution)/shard_map/unpack/pallas_call | solution.py:330

commit v5 on v4

--- a/solution.py
+++ b/solution.py
@@ -19,8 +19,7 @@
 UNIT = 64
 UNITS = TOK // UNIT
 LANES = GROUP * UNIT
-KINDS = MOST_BLOCKS + 1
-TOGETHER = [(n, n + 1) for n in range(1, MOST_BLOCKS)] + [(n, 0) for n in range(KINDS)]
+UNPACK_PARTS = 4
 SHORT = 3 * UNIT
 Q_AT = 0
 G_AT = GROUP * TOK
@@ -39,7 +38,7 @@
 
 
 def pack_kernel(
-    q_ref, k_ref, v_ref, o_ref, g_ref, doc_ref, out_ref, q_buf, k_buf, v_buf, o_buf, g_buf, doc_buf, send, in_sem, kv_sem, sem
+    q_ref, k_ref, v_ref, o_ref, g_ref, doc_ref, out_ref, q_buf, k_buf, v_buf, o_buf, g_buf, doc_buf, send, extras, in_sem, kv_sem, sem, extra_sem
 ):
     whole = [
         pltpu.make_async_copy(k_ref, k_buf, kv_sem.at[0]),
@@ -85,13 +84,22 @@
         own = slice(group * HEAD_WIDTH, (group + 1) * HEAD_WIDTH)
         send[group, K_AT : K_AT + TOK, :] = k_buf[:, own]
         send[group, V_AT : V_AT + TOK, :] = v_buf[:, own]
+        for n, rows in enumerate((pl.ds(Q_AT, G_AT), pl.ds(G_AT, X_AT - G_AT))):
+            departures.append(
+                pltpu.make_async_copy(
+                    send.at[group, rows], out_ref.at[group, rows], sem.at[group, n]
+                )
+            )
+            departures[-1].start()
         delta = jnp.sum(jnp.concatenate(product, axis=0).T, axis=0, keepdims=True)
         delta = jnp.concatenate([delta[:, t * 128 : (t + 1) * 128] for t in range(6)], axis=0)
         high = delta.astype(jnp.bfloat16).astype(jnp.float32)
         extra = jnp.concatenate([high, delta - high, tail], axis=0)
-        send[group, X_AT : X_AT + 16, :] = extra.astype(jnp.bfloat16)
-        departures.append(pltpu.make_async_copy(send.at[group], out_ref.at[group], sem.at[group]))
-        departures[group].start()
+        extras[group] = extra.astype(jnp.bfloat16)
+    departures.append(
+        pltpu.make_async_copy(extras, out_ref.at[:, pl.ds(X_AT, 16)], extra_sem.at[0])
+    )
+    departures[-1].start()
     for copy in departures:
         copy.wait()
 
@@ -117,14 +125,13 @@
         chunk_at = b * TOK + UNIT * lax.broadcasted_iota(jnp.int32, own.shape, 0)
         reach_ref[b] = jnp.max(chunk_at.astype(jnp.float32) - own).astype(jnp.int32)
 
-    def kind_of(i):
-        first_block = first_ref[i] // TOK
+    def case_of(i):
+        unit = first_ref[i] // UNIT
+        first_block = unit // UNITS
         is_short = (i > 0) & (reach_ref[i] <= SHORT - UNIT) & (first_block < i)
-        return jnp.where(is_short, 0, i - first_block + 1)
-
-    def chunks_of(i, kind):
-        short = kind == 0
-        count = kind or 2
+        return i - first_block + 1, unit % UNITS, is_short
+
+    def chunks_of(i, count, skip=0, short=False, over=False):
         start3 = start_ref[i].astype(jnp.int32)
         delta6 = extra_ref[i, 0:6, :] + extra_ref[i, 6:12, :]
         low = i - count + 1
@@ -143,7 +150,8 @@
             return (count - 1) * TOK + (t + 1) * UNIT
 
         def begin(t):
-            return end(t) - SHORT if short else 0
+            ended = over and t > skip
+            return end(t) - SHORT if short or ended else skip * UNIT
 
         def pieces(t):
             edges = list(range(begin(t), end(t), TOK)) + [end(t)]
@@ -223,38 +231,69 @@
         scores_of(0)
         scores_of(1)
         for n in range(count):
-            w[n] = chunks[n][2](s.pop(n))
             if n + 2 < count:
                 scores_of(n + 2)
-            d[n] = chunks[n][1]()
+            w[n] = chunks[n][2](s.pop(n))
             if n > 1:
                 chunks[n - 2][4](*g.pop(n - 2))
             if n > 0:
                 grads(n - 1)
+            d[n] = chunks[n][1]()
         chunks[-2][4](*g.pop(count - 2))
         grads(count - 1)
         chunks[-1][4](*g.pop(count - 1))
 
     def two_blocks(p, carry):
-        first, second = kind_of(2 * p), kind_of(2 * p + 1)
-        code = first * KINDS + second
-        alone = code >= 0
-        for one, two in TOGETHER:
-            match = code == one * KINDS + two
-            alone = alone & jnp.logical_not(match)
-            pl.when(match)(
-                lambda one=one, two=two: run(chunks_of(2 * p, one) + chunks_of(2 * p + 1, two))
-            )
-
-        @pl.when(alone)
+        one, two = 2 * p, 2 * p + 1
+        count1, skip1, short1 = case_of(one)
+        count2, skip2, short2 = case_of(two)
+        long1 = jnp.logical_not(short1)
+        goes_on = (count2 == count1 + 1) & ((count1 == 1) | ((count1 == 3) & (skip1 == skip2)))
+        goes_on = goes_on & long1 & jnp.logical_not(short2)
+        then_short = short2 & (short1 | (count1 == 1) | (count1 == MOST_BLOCKS))
+
+        @pl.when(goes_on)
+        def _():
+            for skip in range(UNITS):
+
+                @pl.when(skip2 == skip)
+                def _(skip=skip):
+                    pl.when(count1 == 1)(
+                        lambda: run(chunks_of(one, 1) + chunks_of(two, 2, skip))
+                    )
+                    pl.when(count1 == 3)(
+                        lambda: run(chunks_of(one, 3, skip) + chunks_of(two, 4, skip))
+                    )
+
+        @pl.when(then_short)
+        def _():
+            def both(first):
+                run(first + chunks_of(two, 2, short=True))
+
+            pl.when(short1)(lambda: both(chunks_of(one, 2, short=True)))
+
+            @pl.when(long1)
+            def _():
+                pl.when(count1 == 1)(lambda: both(chunks_of(one, 1)))
+                for skip in range(UNITS):
+                    pl.when((count1 == MOST_BLOCKS) & (skip1 == skip))(
+                        lambda skip=skip: both(chunks_of(one, MOST_BLOCKS, skip, over=True))
+                    )
+
+        @pl.when(jnp.logical_not(goes_on | then_short))
         def _():
             def one_block(i, carry):
-                kind = kind_of(i)
-                for value in range(KINDS):
-                    pl.when(kind == value)(lambda value=value: run(chunks_of(i, value)))
+                count, skip, short = case_of(i)
+                pl.when(short)(lambda: run(chunks_of(i, 2, short=True)))
+
+                @pl.when(jnp.logical_not(short))
+                def _():
+                    for value in range(1, MOST_BLOCKS + 1):
+                        pl.when(count == value)(lambda value=value: run(chunks_of(i, value)))
+
                 return carry
 
-            lax.fori_loop(2 * p, 2 * p + 2, one_block, 0)
+            lax.fori_loop(one, two + 1, one_block, 0)
 
         return carry
 
@@ -266,25 +305,24 @@
         out_ref[b, at + TOK : at + 2 * TOK, :] = dv_ref[own].astype(jnp.bfloat16)
 
 
-def unpack_kernel(back_ref, dq_ref, dk_ref, dv_ref, sem):
+def unpack_kernel(back_ref, dq_ref, dk_ref, dv_ref, dq_buf, dk_buf, dv_buf, sem):
     copies = []
-
-    def send(group, at, ref, column):
-        copies.append(
-            pltpu.make_async_copy(
-                back_ref.at[group, pl.ds(at, TOK)],
-                ref.at[:, column * HEAD_WIDTH : (column + 1) * HEAD_WIDTH],
-                sem.at[len(copies)],
-            )
-        )
-
-    for group in range(KEY_VALUE_HEADS):
-        for h in range(GROUP):
-            send(group, h * TOK, dq_ref, group * GROUP + h)
-        send(group, GROUP * TOK, dk_ref, group)
-        send(group, (GROUP + 1) * TOK, dv_ref, group)
-    for copy in copies:
-        copy.start()
+    for part in range(UNPACK_PARTS):
+        size = TOK // UNPACK_PARTS
+        rows = slice(part * size, (part + 1) * size)
+        for group in range(KEY_VALUE_HEADS):
+            for h in range(GROUP):
+                head = group * GROUP + h
+                at = h * TOK + part * size
+                cols = slice(head * HEAD_WIDTH, (head + 1) * HEAD_WIDTH)
+                dq_buf[rows, cols] = back_ref[group, at : at + size, :]
+            cols = slice(group * HEAD_WIDTH, (group + 1) * HEAD_WIDTH)
+            for n, buf in enumerate((dk_buf, dv_buf)):
+                at = (GROUP + n) * TOK + part * size
+                buf[rows, cols] = back_ref[group, at : at + size, :]
+        for n, (buf, ref) in enumerate(((dq_buf, dq_ref), (dk_buf, dk_ref), (dv_buf, dv_ref))):
+            copies.append(pltpu.make_async_copy(buf.at[rows], ref.at[rows], sem.at[part, n]))
+            copies[-1].start()
     for copy in copies:
         copy.wait()
 
@@ -303,10 +341,12 @@
             pltpu.VMEM(outputs.shape, jnp.bfloat16),
             pltpu.VMEM(output_gradient.shape, jnp.bfloat16),
             pltpu.VMEM((1, TOK), jnp.int32),
-            pltpu.VMEM((KEY_VALUE_HEADS, SEND_ROWS, 128), jnp.bfloat16),
+            pltpu.VMEM((KEY_VALUE_HEADS, X_AT, 128), jnp.bfloat16),
+            pltpu.VMEM((KEY_VALUE_HEADS, 16, 128), jnp.bfloat16),
             pltpu.SemaphoreType.DMA((3, KEY_VALUE_HEADS)),
             pltpu.SemaphoreType.DMA((3,)),
-            pltpu.SemaphoreType.DMA((KEY_VALUE_HEADS,)),
+            pltpu.SemaphoreType.DMA((KEY_VALUE_HEADS, 2)),
+            pltpu.SemaphoreType.DMA((1,)),
         ],
         compiler_params=pltpu.CompilerParams(vmem_limit_bytes=62 * 2**20),
         name="pack",
@@ -329,14 +369,19 @@
     back = lax.all_to_all(result, "blk", 0, 0, tiled=True)
     return pl.pallas_call(
         unpack_kernel,
-        in_specs=[pl.BlockSpec(memory_space=pl.ANY)],
+        in_specs=[pl.BlockSpec(memory_space=pltpu.VMEM)],
         out_specs=[hbm] * 3,
         out_shape=[
             jax.ShapeDtypeStruct(queries.shape, jnp.bfloat16),
             jax.ShapeDtypeStruct(keys.shape, jnp.bfloat16),
             jax.ShapeDtypeStruct(values.shape, jnp.bfloat16),
         ],
-        scratch_shapes=[pltpu.SemaphoreType.DMA((QUERY_HEADS + 2 * KEY_VALUE_HEADS,))],
+        scratch_shapes=[
+            pltpu.VMEM(queries.shape, jnp.bfloat16),
+            pltpu.VMEM(keys.shape, jnp.bfloat16),
+            pltpu.VMEM(values.shape, jnp.bfloat16),
+            pltpu.SemaphoreType.DMA((UNPACK_PARTS, 3)),
+        ],
         compiler_params=pltpu.CompilerParams(vmem_limit_bytes=32 * 2**20),
         name="unpack",
     )(back)

time: 101 us -> 99.9 us (0.989)
  Pallas kernels: 16.4 us -> 14.9 us
    pallas_call x1, Pallas kernels: 9.35 us -> 8.05 us  [local(): pl.pallas_call(attention_kernel, out_shape=jax.ShapeDtypeStruct((BLOCKS,...]
where the time goes in v5:
time: 99.9 us; the launch traced here: 99.7 us
  blocking collectives  84.1 us (84%)
  Pallas kernels  14.9 us (15%)
    all_to_all x1, blocking collectives, local(): payload = lax.all_to_all(packed, 'blk', 0, 0, tiled=True)  53.4 us
    all_to_all x1, blocking collectives, local(): back = lax.all_to_all(result, 'blk', 0, 0, tiled=True)  30.7 us
    pallas_call x1, Pallas kernels, local(): pl.pallas_call(attention_kernel, out_shape=jax.ShapeDtypeStruct((BLOCKS,...  8.05 us
    pallas_call x1, Pallas kernels, local(): pl.pallas_call(pack_kernel, in_specs=[hbm] * 6, out_specs=hbm, out_shape=...  5.29 us

profile of v5, /device:TPU:0, one launch (start us, length us, event | category | flops | bytes accessed | tf_op | source)
XLA Modules:
  0.0 99.7 jit_solution(3685353149343401656)
XLA Ops:
  0.6 5.3 %pack.1 = bf16[8,1936,128]{2,1,0:T(8,128)(2,1)} custom-call(bf16[192,4096]{1,0:T(8,128)(2,1)} %q_ref.1, bf16[192,1024]{1,0:T(8,128)(2,1)} %k_ref.1, bf16[192,1024]{1,0:T(8,128)(2,1)} %v_ref.1, bf16[192,4096]{1,0:T(8,128)(2,1)} %o_ref.1, bf16[192,4096]{1,0:T(8,128)(2,1)} %g_ref.1, s32[1,192]{1,0:T(1,128)} %bitcast.1), custom_call_target="tpu_custom_call" | custom-call | tf_op jit(solution)/shard_map/pack/pallas_call | solution.py:332
  5.9 53.4 %all_to_all.10.pay_ref = bf16[8,1936,128]{2,1,0:T(8,128)(2,1)S(1)} all-to-all(bf16[8,1936,128]{2,1,0:T(8,128)(2,1)} %pack.1), channel_id=1, replica_groups=mesh['dp'=16,'blk'=8] {'blk'}, dimensions={0} | all-to-all | bytes 7929856 | tf_op jit(solution)/shard_map/all_to_all | solution.py:354
  59.4 8.0 %attention.1 = bf16[8,1152,128]{2,1,0:T(8,128)(2,1)S(1)} custom-call(bf16[8,1936,128]{2,1,0:T(8,128)(2,1)S(1)} %all_to_all.10.pay_ref), custom_call_target="tpu_custom_call" | custom-call | tf_op jit(solution)/shard_map/attention/pallas_call | solution.py:355
  67.4 30.7 %all_to_all.11.back_ref = bf16[8,1152,128]{2,1,0:T(8,128)(2,1)S(1)} all-to-all(bf16[8,1152,128]{2,1,0:T(8,128)(2,1)S(1)} %attention.1), channel_id=1, replica_groups=mesh['dp'=16,'blk'=8] {'blk'}, dimensions={0} | all-to-all | bytes 4718592 | tf_op jit(solution)/shard_map/all_to_all | solution.py:369
  98.1 1.6 %unpack.1 = (bf16[192,4096]{1,0:T(8,128)(2,1)}, bf16[192,1024]{1,0:T(8,128)(2,1)}, bf16[192,1024]{1,0:T(8,128)(2,1)}) custom-call(bf16[8,1152,128]{2,1,0:T(8,128)(2,1)S(1)} %all_to_all.11.back_ref), custom_call_target="tpu_custom_call" | custom-call | tf_op jit(solution)/shard_map/unpack/pallas_call | solution.py:370

commit v6 on v5

--- a/solution.py
+++ b/solution.py
@@ -60,16 +60,17 @@
             for copy in whole:
                 copy.start()
     departures = []
+
+    def depart(group, n, first, last):
+        rows = pl.ds(first, last - first)
+        departures.append(
+            pltpu.make_async_copy(send.at[group, rows], out_ref.at[group, rows], sem.at[group, n])
+        )
+        departures[-1].start()
+
     for group in range(KEY_VALUE_HEADS):
         for copy in arrivals[group]:
             copy.wait()
-        if group == 0:
-            for copy in whole:
-                copy.wait()
-            doc = doc_buf[...].astype(jnp.float32)
-            tail = [doc[:, t * UNIT : (t + 1) * UNIT] for t in range(UNITS)]
-            tail = [jnp.concatenate([part, part], axis=1) for part in tail]
-            tail = jnp.concatenate(tail + [jnp.zeros((1, 128), jnp.float32)], axis=0)
         product = []
         for t in range(UNITS):
             rows = slice(t * UNIT, (t + 1) * UNIT)
@@ -81,16 +82,19 @@
                 send[group, Q_AT + at : Q_AT + at + UNIT, :] = q_buf[rows, cols]
                 send[group, G_AT + at : G_AT + at + UNIT, :] = g
                 product.append(g.astype(jnp.float32) * o_buf[rows, cols].astype(jnp.float32))
+        depart(group, 0, Q_AT, G_AT)
+        depart(group, 1, G_AT, K_AT)
+        if group == 0:
+            for copy in whole:
+                copy.wait()
+            doc = doc_buf[...].astype(jnp.float32)
+            tail = [doc[:, t * UNIT : (t + 1) * UNIT] for t in range(UNITS)]
+            tail = [jnp.concatenate([part, part], axis=1) for part in tail]
+            tail = jnp.concatenate(tail + [jnp.zeros((1, 128), jnp.float32)], axis=0)
         own = slice(group * HEAD_WIDTH, (group + 1) * HEAD_WIDTH)
         send[group, K_AT : K_AT + TOK, :] = k_buf[:, own]
         send[group, V_AT : V_AT + TOK, :] = v_buf[:, own]
-        for n, rows in enumerate((pl.ds(Q_AT, G_AT), pl.ds(G_AT, X_AT - G_AT))):
-            departures.append(
-                pltpu.make_async_copy(
-                    send.at[group, rows], out_ref.at[group, rows], sem.at[group, n]
-                )
-            )
-            departures[-1].start()
+        depart(group, 2, K_AT, X_AT)
         delta = jnp.sum(jnp.concatenate(product, axis=0).T, axis=0, keepdims=True)
         delta = jnp.concatenate([delta[:, t * 128 : (t + 1) * 128] for t in range(6)], axis=0)
         high = delta.astype(jnp.bfloat16).astype(jnp.float32)
@@ -345,7 +349,7 @@
             pltpu.VMEM((KEY_VALUE_HEADS, 16, 128), jnp.bfloat16),
             pltpu.SemaphoreType.DMA((3, KEY_VALUE_HEADS)),
             pltpu.SemaphoreType.DMA((3,)),
-            pltpu.SemaphoreType.DMA((KEY_VALUE_HEADS, 2)),
+            pltpu.SemaphoreType.DMA((KEY_VALUE_HEADS, 3)),
             pltpu.SemaphoreType.DMA((1,)),
         ],
         compiler_params=pltpu.CompilerParams(vmem_limit_bytes=62 * 2**20),

time: 99.9 us -> 100 us (level)
  no operation moved by 1% of the time
where the time goes in v6:
time: 100 us; the launch traced here: 99.9 us
  blocking collectives  84 us (84%)
  Pallas kernels  15.2 us (15%)
    all_to_all x1, blocking collectives, local(): payload = lax.all_to_all(packed, 'blk', 0, 0, tiled=True)  53.4 us
    all_to_all x1, blocking collectives, local(): back = lax.all_to_all(result, 'blk', 0, 0, tiled=True)  30.6 us
    pallas_call x1, Pallas kernels, local(): pl.pallas_call(attention_kernel, out_shape=jax.ShapeDtypeStruct((BLOCKS,...  8.17 us
    pallas_call x1, Pallas kernels, local(): pl.pallas_call(pack_kernel, in_specs=[hbm] * 6, out_specs=hbm, out_shape=...  5.48 us

profile of v6, /device:TPU:0, one launch (start us, length us, event | category | flops | bytes accessed | tf_op | source)
XLA Modules:
  0.0 99.9 jit_solution(2895277863814927299)
XLA Ops:
  0.6 5.5 %pack.1 = bf16[8,1936,128]{2,1,0:T(8,128)(2,1)} custom-call(bf16[192,4096]{1,0:T(8,128)(2,1)} %q_ref.1, bf16[192,1024]{1,0:T(8,128)(2,1)} %k_ref.1, bf16[192,1024]{1,0:T(8,128)(2,1)} %v_ref.1, bf16[192,4096]{1,0:T(8,128)(2,1)} %o_ref.1, bf16[192,4096]{1,0:T(8,128)(2,1)} %g_ref.1, s32[1,192]{1,0:T(1,128)} %bitcast.1), custom_call_target="tpu_custom_call" | custom-call | tf_op jit(solution)/shard_map/pack/pallas_call | solution.py:336
  6.1 53.4 %all_to_all.10.pay_ref = bf16[8,1936,128]{2,1,0:T(8,128)(2,1)S(1)} all-to-all(bf16[8,1936,128]{2,1,0:T(8,128)(2,1)} %pack.1), channel_id=1, replica_groups=mesh['dp'=16,'blk'=8] {'blk'}, dimensions={0} | all-to-all | bytes 7929856 | tf_op jit(solution)/shard_map/all_to_all | solution.py:358
  59.5 8.2 %attention.1 = bf16[8,1152,128]{2,1,0:T(8,128)(2,1)S(1)} custom-call(bf16[8,1936,128]{2,1,0:T(8,128)(2,1)S(1)} %all_to_all.10.pay_ref), custom_call_target="tpu_custom_call" | custom-call | tf_op jit(solution)/shard_map/attention/pallas_call | solution.py:359
  67.7 30.6 %all_to_all.11.back_ref = bf16[8,1152,128]{2,1,0:T(8,128)(2,1)S(1)} all-to-all(bf16[8,1152,128]{2,1,0:T(8,128)(2,1)S(1)} %attention.1), channel_id=1, replica_groups=mesh['dp'=16,'blk'=8] {'blk'}, dimensions={0} | all-to-all | bytes 4718592 | tf_op jit(solution)/shard_map/all_to_all | solution.py:373
  98.3 1.6 %unpack.1 = (bf16[192,4096]{1,0:T(8,128)(2,1)}, bf16[192,1024]{1,0:T(8,128)(2,1)}, bf16[192,1024]{1,0:T(8,128)(2,1)}) custom-call(bf16[8,1152,128]{2,1,0:T(8,128)(2,1)S(1)} %all_to_all.11.back_ref), custom_call_target="tpu_custom_call" | custom-call | tf_op jit(solution)/shard_map/unpack/pallas_call | solution.py:374
